TPU v7x, 32 devices: a whole 2x2x4 slice. The times are simulated.
32 devices in a mesh: win: 4 (over y, x), blk: 8 (over z, core).
Axes of the slice: x: 2, y: 2, z: 4, core: 2. Of those that a mesh axis runs over, the one named last changes fastest.
Arguments:
- inputs: bfloat16 [8, 1024, 768], P('win', 'blk'), may hold values from -6 to 6
- species: int32 [8], replicated, may hold values from 0 to 3, as said below
- random_blocks: int32 [16, 12, 3], replicated, may hold values from 1 to 14, as said below
- qkv_weight: bfloat16 [768, 2304], replicated, may hold values from -0.21875 to 0.21875
- q_bias: float32 [768], replicated, may hold values from -3 to 3
- v_bias: float32 [768], replicated, may hold values from -0.12 to 0.12
- out_weight: bfloat16 [768, 768], replicated, may hold values from -2.5 to 2.5
- out_bias: float32 [768], replicated, may hold values from -1.2 to 1.2
- norm1_gain: float32 [768], replicated, may hold values from 0.5 to 1.5
- norm1_bias: float32 [768], replicated, may hold values from -1.2 to 1.2
- norm2_gain: float32 [768], replicated, may hold values from 0.5 to 1.5
- norm2_bias: float32 [768], replicated, may hold values from -1.2 to 1.2
- ffn_in_weight: bfloat16 [768, 3072], replicated, may hold values from -0.21875 to 0.21875
- ffn_in_bias: float32 [3072], replicated, may hold values from -1.2 to 1.2
- ffn_out_weight: bfloat16 [3072, 768], replicated, may hold values from -0.15625 to 0.15625
- ffn_out_bias: float32 [768], replicated, may hold values from -1.2 to 1.2
- cotangent: bfloat16 [16, 1024, 768], P('win', 'blk'), may hold values from -6 to 6
Outputs:
- result: bfloat16 [16, 1024, 768], P('win', 'blk')
- input_grad: bfloat16 [8, 1024, 768], P('win', 'blk')
- qkv_weight_grad: float32 [768, 2304], replicated
- q_bias_grad: float32 [768], replicated
- v_bias_grad: float32 [768], replicated
- out_weight_grad: float32 [768, 768], replicated
- out_bias_grad: float32 [768], replicated
- norm1_gain_grad: float32 [768], replicated
- norm1_bias_grad: float32 [768], replicated
- norm2_gain_grad: float32 [768], replicated
- norm2_bias_grad: float32 [768], replicated
- ffn_in_weight_grad: float32 [768, 3072], replicated
- ffn_in_bias_grad: float32 [3072], replicated
- ffn_out_weight_grad: float32 [3072, 768], replicated
- ffn_out_bias_grad: float32 [768], replicated
Inputs may be any that keep to these rules, and one draw needn't show every extreme that they name: One species group, drawn from the seed, holds exactly 4 windows and none holds more; the other groups share the rest as evenly as possible. `random_blocks`: take the blocks in groups of 2 consecutive ones. For each query block and head the 3 blocks lie in different groups, none in the query block's own group, and none is the first or last block. Of the 72 picks of one group's query blocks, at most (78) // 7 lie in any one other group, and the group just before it (the last group before the first) receives exactly that many.
All inputs are finite; a program needn't handle non-finite values.
Results may differ from a plain program's by a relative error of at most 0.013.
Values may be sent and summed in bfloat16 or wider, within the bound.
No kernel may reach another device: no remote copies, remote signals or barrier semaphores. Data moves between devices by JAX's collectives and lax.ppermute only.
A program may use at most 320 MiB of HBM per device.

v0:
```python
import jax
import jax.numpy as jnp
from jax import lax
from jax.sharding import PartitionSpec as P

HEADS = 12
HD = 64
BS = 64
RAND = 3


NORM_EPS = 1e-05
SCORE_SCALE = 0.125
MASKED_SCORE = -1e30


def padded(block, sides, width):
    for axis, dim in sides:
        count = lax.axis_size(axis)
        forward = [(i, i + 1) for i in range(count - 1)]
        backward = [(target, source) for source, target in forward]
        low = lax.ppermute(
            lax.slice_in_dim(block, block.shape[dim] - width, None, axis=dim), axis, forward
        )
        high = lax.ppermute(lax.slice_in_dim(block, 0, width, axis=dim), axis, backward)
        block = jnp.concatenate([low, block, high], axis=dim)
    return block


def joined(array, axis, combine):
    everything = jax.tree.map(lambda part: lax.all_gather(part, axis), array)
    leading = jax.tree.map(lambda part: part[0], everything)

    def turn(k, so_far):
        return combine(so_far, jax.tree.map(lambda part: part[k], everything))

    return lax.fori_loop(1, lax.axis_size(axis), turn, leading)


def layer_norm(values, gain_vec, bias_vec):
    average = jnp.mean(values, axis=-1, keepdims=True)
    centred = values - average
    spread = jnp.mean(centred * centred, axis=-1, keepdims=True)
    return centred * lax.rsqrt(spread + NORM_EPS) * gain_vec + bias_vec


def gelu_exact(values):
    return jax.nn.gelu(values, approximate=False)


def slot_mask(block_ids, block_total):
    always = jnp.ones(block_ids.shape, dtype=jnp.bool_)
    columns = [
        block_ids >= 1,
        always,
        block_ids <= block_total - 2,
        block_ids >= 2,
        block_ids <= block_total - 3,
    ] + [always] * RAND
    return jnp.stack(columns, axis=1)


def join_stats(earlier, later):
    row_top = jnp.maximum(earlier[0], later[0])
    return (
        row_top,
        earlier[1] * jnp.exp(earlier[0] - row_top) + later[1] * jnp.exp(later[0] - row_top),
    )


def rank_within(species):
    window = jnp.arange(species.shape[0], dtype=jnp.int32)
    same_group = species[:, None] == species[None, :]
    earlier = window[None, :] < window[:, None]
    return jnp.sum((same_group & earlier).astype(jnp.int32), axis=1)


def group_buffer(local_rows, species, slot_rank, group_index, groups, slot_count):
    count_here = local_rows.shape[0]
    mine_group = lax.dynamic_slice_in_dim(species, group_index * count_here, count_here)
    mine_rank = lax.dynamic_slice_in_dim(slot_rank, group_index * count_here, count_here)
    target = (mine_group[None, None, :] == jnp.arange(groups, dtype=jnp.int32)[:, None, None]) & (
        mine_rank[None, None, :] == jnp.arange(slot_count, dtype=jnp.int32)[None, :, None]
    )
    return jnp.einsum(
        "gkj,jtd->gktd", target.astype(jnp.bfloat16), local_rows, preferred_element_type=jnp.float32
    ).astype(jnp.bfloat16)


def anchor_buffer(grouped, species, slot_rank, group_index, groups, per_group):
    all_groups = species.reshape(groups, per_group)
    all_ranks = slot_rank.reshape(groups, per_group)
    target = (all_groups == group_index)[:, :, None] & (
        all_ranks[:, :, None] == jnp.arange(grouped.shape[0], dtype=jnp.int32)[None, None, :]
    )
    return jnp.einsum(
        "cjk,ktd->cjtd", target.astype(jnp.bfloat16), grouped, preferred_element_type=jnp.float32
    ).astype(jnp.bfloat16)


def sparse_scores(query_blocks, near_key, end_key, far_key, allowed):
    near_part = jnp.einsum(
        "sjqhd,sjkhd->sjhqk", query_blocks, near_key, preferred_element_type=jnp.float32
    )
    end_part = jnp.einsum(
        "sjqhd,skhd->sjhqk", query_blocks, end_key, preferred_element_type=jnp.float32
    )
    far_part = jnp.einsum(
        "sjqhd,sjhkd->sjhqk", query_blocks, far_key, preferred_element_type=jnp.float32
    )
    scores = jnp.concatenate([near_part, end_part, far_part], axis=-1) * SCORE_SCALE
    return jnp.where(allowed, scores, MASKED_SCORE)


def layer_pass(tokens, upstream, live_slots, random_picks, weights):
    (
        w_qkv,
        bias_q,
        bias_v,
        w_out,
        bias_out,
        gain_one,
        shift_one,
        gain_two,
        shift_two,
        w_in,
        bias_in,
        w_down,
        bias_down,
    ) = weights
    windows, tok_dev, model_width = tokens.shape
    per_dev = tok_dev // BS
    row_count = windows * tok_dev
    near_stop = 3 * BS
    far_start = 5 * BS
    blk_index = lax.axis_index("blk")
    blk_count = lax.axis_size("blk")
    total_blocks = blk_count * per_dev
    block_ids = blk_index * per_dev + jnp.arange(per_dev, dtype=jnp.int32)
    is_first = blk_index == 0
    is_final = blk_index == blk_count - 1
    local_picks = lax.dynamic_slice_in_dim(random_picks, blk_index * per_dev, per_dev, 0)
    allowed = jnp.repeat(slot_mask(block_ids, total_blocks), BS, axis=1)[None, :, None, None, :]
    token_float = tokens.astype(jnp.float32)
    normed, norm_one_back = jax.vjp(layer_norm, token_float, gain_one, shift_one)
    normed_low = normed.astype(jnp.bfloat16).reshape(row_count, model_width)
    mixed_qkv = jnp.dot(normed_low, w_qkv, preferred_element_type=jnp.float32).reshape(
        windows, tok_dev, 3 * model_width
    )
    query_low = (mixed_qkv[..., :model_width] + bias_q).astype(jnp.bfloat16)
    key_low = mixed_qkv[..., model_width : 2 * model_width].astype(jnp.bfloat16)
    value_low = (mixed_qkv[..., 2 * model_width :] + bias_v).astype(jnp.bfloat16)
    key_value = jnp.concatenate([key_low, value_low], axis=-1)
    own_rows = jnp.concatenate([query_low, key_low, value_low], axis=-1)
    end_rows = jnp.stack(
        [
            jnp.where(is_first, own_rows[:, :BS], jnp.zeros((), jnp.bfloat16)),
            jnp.where(is_final, own_rows[:, tok_dev - BS :], jnp.zeros((), jnp.bfloat16)),
        ],
        axis=1,
    )
    shared = lax.psum(end_rows.astype(jnp.float32), "blk").astype(jnp.bfloat16)
    end_query = shared[..., :model_width].reshape(windows, 2, BS, HEADS, HD)
    end_key = shared[..., model_width : 2 * model_width].reshape(windows, 2 * BS, HEADS, HD)
    end_value = shared[..., 2 * model_width :].reshape(windows, 2 * BS, HEADS, HD)
    extended = padded(key_value, (("blk", 1),), BS)
    ext_blocks = extended.reshape(windows, per_dev + 2, BS, 2, HEADS, HD)
    near_kv = jnp.stack(
        [ext_blocks[:, offset : offset + per_dev] for offset in range(3)], axis=2
    ).reshape(windows, per_dev, 3 * BS, 2, HEADS, HD)
    near_key = near_kv[:, :, :, 0]
    near_value = near_kv[:, :, :, 1]
    row_index = local_picks[..., None] * BS + jnp.arange(BS, dtype=jnp.int32)
    flat_index = (row_index[..., None] * 2 + jnp.arange(2, dtype=jnp.int32)) * HEADS + jnp.arange(
        HEADS, dtype=jnp.int32
    )[None, :, None, None, None]

    def fetch_far(window_kv):
        whole_kv = lax.all_gather(window_kv, "blk", axis=0, tiled=True)
        return jnp.take(whole_kv.reshape(-1, HD), flat_index, axis=0)

    far_kv = lax.map(fetch_far, key_value)
    far_key = far_kv[..., 0, :].reshape(windows, per_dev, HEADS, RAND * BS, HD)
    far_value = far_kv[..., 1, :].reshape(windows, per_dev, HEADS, RAND * BS, HD)
    query_blocks = query_low.reshape(windows, per_dev, BS, HEADS, HD)
    scores = sparse_scores(query_blocks, near_key, end_key, far_key, allowed)
    row_top = jnp.max(scores, axis=-1, keepdims=True)
    log_total = row_top + jnp.log(jnp.sum(jnp.exp(scores - row_top), axis=-1, keepdims=True))
    probs_low = jnp.exp(scores - log_total).astype(jnp.bfloat16)
    sparse_out = jnp.einsum(
        "sjhqk,sjkhd->sjqhd",
        probs_low[..., :near_stop],
        near_value,
        preferred_element_type=jnp.float32,
    )
    sparse_out = sparse_out + jnp.einsum(
        "sjhqk,skhd->sjqhd",
        probs_low[..., near_stop:far_start],
        end_value,
        preferred_element_type=jnp.float32,
    )
    sparse_out = sparse_out + jnp.einsum(
        "sjhqk,sjhkd->sjqhd",
        probs_low[..., far_start:],
        far_value,
        preferred_element_type=jnp.float32,
    )
    key_here = key_low.reshape(windows, tok_dev, HEADS, HD)
    value_here = value_low.reshape(windows, tok_dev, HEADS, HD)
    wide_scores = (
        jnp.einsum("sgqhd,skhd->sghqk", end_query, key_here, preferred_element_type=jnp.float32)
        * SCORE_SCALE
    )
    local_top = jnp.max(wide_scores, axis=-1)
    local_total = jnp.sum(jnp.exp(wide_scores - local_top[..., None]), axis=-1)
    wide_top, wide_total = joined((local_top, local_total), "blk", join_stats)
    wide_log = (wide_top + jnp.log(wide_total))[..., None]
    wide_probs = jnp.exp(wide_scores - wide_log)
    wide_low = wide_probs.astype(jnp.bfloat16)
    part_out = jnp.einsum(
        "sghqk,skhd->sgqhd", wide_low, value_here, preferred_element_type=jnp.float32
    )
    part_exact = jnp.einsum(
        "sghqk,skhd->sgqhd",
        wide_probs,
        value_here.astype(jnp.float32),
        precision=lax.Precision.HIGHEST,
    )
    end_out, end_exact = lax.psum((part_out, part_exact), "blk")
    head_rows = sparse_out.reshape(windows, tok_dev, model_width)
    first_rows = end_out[:, 0].reshape(windows, BS, model_width)
    final_rows = end_out[:, 1].reshape(windows, BS, model_width)
    head_rows = head_rows.at[:, :BS].set(jnp.where(is_first, first_rows, head_rows[:, :BS]))
    head_rows = head_rows.at[:, tok_dev - BS :].set(
        jnp.where(is_final, final_rows, head_rows[:, tok_dev - BS :])
    )
    heads_low = head_rows.astype(jnp.bfloat16).reshape(row_count, model_width)
    attn_term = jnp.dot(heads_low, w_out, preferred_element_type=jnp.float32) + bias_out
    residual = token_float + attn_term.reshape(windows, tok_dev, model_width)
    second, norm_two_back = jax.vjp(layer_norm, residual, gain_two, shift_two)
    second_low = second.astype(jnp.bfloat16).reshape(row_count, model_width)
    hidden = jnp.dot(second_low, w_in, preferred_element_type=jnp.float32) + bias_in
    activated, gelu_back = jax.vjp(gelu_exact, hidden)
    act_low = activated.astype(jnp.bfloat16)
    output = residual + (
        jnp.dot(act_low, w_down, preferred_element_type=jnp.float32) + bias_down
    ).reshape(windows, tok_dev, model_width)
    live = live_slots[:, None, None]
    result = jnp.where(live, output, 0.0).astype(jnp.bfloat16)
    grad_low = jnp.where(live, upstream, jnp.zeros((), jnp.bfloat16))
    grad_flat = grad_low.reshape(row_count, model_width)
    grad_down = jnp.einsum("rf,rd->fd", act_low, grad_flat, preferred_element_type=jnp.float32)
    grad_bias_down = jnp.sum(grad_flat.astype(jnp.float32), axis=0)
    grad_act = jnp.einsum("rd,fd->rf", grad_flat, w_down, preferred_element_type=jnp.float32)
    (grad_hidden,) = gelu_back(grad_act)
    hidden_low = grad_hidden.astype(jnp.bfloat16)
    grad_in = jnp.einsum("rd,rf->df", second_low, hidden_low, preferred_element_type=jnp.float32)
    grad_bias_in = jnp.sum(hidden_low.astype(jnp.float32), axis=0)
    grad_second = jnp.einsum(
        "rf,df->rd", hidden_low, w_in, preferred_element_type=jnp.float32
    ).reshape(windows, tok_dev, model_width)
    grad_resid_norm, grad_gain_two, grad_shift_two = norm_two_back(grad_second)
    grad_resid = grad_low.astype(jnp.float32) + grad_resid_norm
    resid_low = grad_resid.astype(jnp.bfloat16).reshape(row_count, model_width)
    grad_out = jnp.einsum("rd,re->de", heads_low, resid_low, preferred_element_type=jnp.float32)
    grad_bias_out = jnp.sum(resid_low.astype(jnp.float32), axis=0)
    grad_heads = (
        jnp.einsum("re,de->rd", resid_low, w_out, preferred_element_type=jnp.float32)
        .astype(jnp.bfloat16)
        .reshape(windows, tok_dev, model_width)
    )
    heads_first = grad_heads[:, :BS].reshape(windows, BS, HEADS, HD).astype(jnp.float32)
    heads_final = grad_heads[:, tok_dev - BS :].reshape(windows, BS, HEADS, HD).astype(jnp.float32)
    delta_first = jnp.sum(heads_first * end_exact[:, 0], axis=-1)
    delta_final = jnp.sum(heads_final * end_exact[:, 1], axis=-1)
    grad_ends = jnp.stack(
        [jnp.where(is_first, heads_first, 0.0), jnp.where(is_final, heads_final, 0.0)], axis=1
    )
    delta_ends = jnp.stack(
        [jnp.where(is_first, delta_first, 0.0), jnp.where(is_final, delta_final, 0.0)], axis=1
    )
    wide_grad, wide_delta = lax.psum((grad_ends, delta_ends), "blk")
    wide_grad_low = wide_grad.astype(jnp.bfloat16)
    keep_block = (block_ids != 0) & (block_ids != total_blocks - 1)
    grad_sparse = jnp.where(
        keep_block[None, :, None, None, None],
        grad_heads.reshape(windows, per_dev, BS, HEADS, HD),
        jnp.zeros((), jnp.bfloat16),
    )
    scores = sparse_scores(query_blocks, near_key, end_key, far_key, allowed)
    probs = jnp.exp(scores - log_total)
    probs_low = probs.astype(jnp.bfloat16)
    grad_probs = jnp.concatenate(
        [
            jnp.einsum(
                "sjqhd,sjkhd->sjhqk", grad_sparse, near_value, preferred_element_type=jnp.float32
            ),
            jnp.einsum(
                "sjqhd,skhd->sjhqk", grad_sparse, end_value, preferred_element_type=jnp.float32
            ),
            jnp.einsum(
                "sjqhd,sjhkd->sjhqk", grad_sparse, far_value, preferred_element_type=jnp.float32
            ),
        ],
        axis=-1,
    )
    row_delta = jnp.sum(probs * grad_probs, axis=-1, keepdims=True)
    grad_scores = (probs * (grad_probs - row_delta)).astype(jnp.bfloat16)
    scores_near = grad_scores[..., :near_stop]
    scores_end = grad_scores[..., near_stop:far_start]
    scores_far = grad_scores[..., far_start:]
    grad_query = jnp.einsum(
        "sjhqk,sjkhd->sjqhd", scores_near, near_key, preferred_element_type=jnp.float32
    )
    grad_query = grad_query + jnp.einsum(
        "sjhqk,skhd->sjqhd", scores_end, end_key, preferred_element_type=jnp.float32
    )
    grad_query = (
        grad_query
        + jnp.einsum("sjhqk,sjhkd->sjqhd", scores_far, far_key, preferred_element_type=jnp.float32)
    ) * SCORE_SCALE
    grad_near_key = (
        jnp.einsum(
            "sjhqk,sjqhd->sjkhd", scores_near, query_blocks, preferred_element_type=jnp.float32
        )
        * SCORE_SCALE
    )
    grad_near_value = jnp.einsum(
        "sjhqk,sjqhd->sjkhd",
        probs_low[..., :near_stop],
        grad_sparse,
        preferred_element_type=jnp.float32,
    )
    grad_end_key = (
        jnp.einsum(
            "sjhqk,sjqhd->skhd", scores_end, query_blocks, preferred_element_type=jnp.float32
        )
        * SCORE_SCALE
    )
    grad_end_value = jnp.einsum(
        "sjhqk,sjqhd->skhd",
        probs_low[..., near_stop:far_start],
        grad_sparse,
        preferred_element_type=jnp.float32,
    )
    grad_far_key = (
        jnp.einsum(
            "sjhqk,sjqhd->sjhkd", scores_far, query_blocks, preferred_element_type=jnp.float32
        )
        * SCORE_SCALE
    )
    grad_far_value = jnp.einsum(
        "sjhqk,sjqhd->sjhkd",
        probs_low[..., far_start:],
        grad_sparse,
        preferred_element_type=jnp.float32,
    )
    wide_scores = (
        jnp.einsum("sgqhd,skhd->sghqk", end_query, key_here, preferred_element_type=jnp.float32)
        * SCORE_SCALE
    )
    wide_probs = jnp.exp(wide_scores - wide_log)
    wide_low = wide_probs.astype(jnp.bfloat16)
    grad_wide = jnp.einsum(
        "sgqhd,skhd->sghqk", wide_grad_low, value_here, preferred_element_type=jnp.float32
    )
    wide_rows = jnp.transpose(wide_delta, (0, 1, 3, 2))[..., None]
    grad_wide_low = (wide_probs * (grad_wide - wide_rows)).astype(jnp.bfloat16)
    grad_end_query = (
        jnp.einsum("sghqk,skhd->sgqhd", grad_wide_low, key_here, preferred_element_type=jnp.float32)
        * SCORE_SCALE
    )
    grad_key_here = (
        jnp.einsum(
            "sghqk,sgqhd->skhd", grad_wide_low, end_query, preferred_element_type=jnp.float32
        )
        * SCORE_SCALE
    )
    grad_value_here = jnp.einsum(
        "sghqk,sgqhd->skhd", wide_low, wide_grad_low, preferred_element_type=jnp.float32
    )
    packed = jnp.concatenate(
        [
            grad_end_query.reshape(windows, 2, BS, model_width),
            grad_end_key.reshape(windows, 2, BS, model_width),
            grad_end_value.reshape(windows, 2, BS, model_width),
        ],
        axis=-1,
    )
    summed = lax.psum(packed, "blk")
    grad_near = jnp.stack([grad_near_key, grad_near_value], axis=3).reshape(
        windows, per_dev, 3, BS, 2 * model_width
    )
    grad_ext = jnp.zeros((windows, tok_dev + 2 * BS, 2 * model_width), jnp.float32)
    for offset in range(3):
        piece = grad_near[:, :, offset].reshape(windows, tok_dev, 2 * model_width)
        grad_ext = grad_ext.at[:, offset * BS : offset * BS + tok_dev].add(piece)
    rim_parts = jnp.concatenate([grad_ext[:, :BS], grad_ext[:, tok_dev + BS :]], axis=1)
    rim_back = padded(rim_parts, (("blk", 1),), BS)
    grad_far = jnp.stack(
        [
            grad_far_key.reshape(windows, per_dev, HEADS, RAND, BS, HD),
            grad_far_value.reshape(windows, per_dev, HEADS, RAND, BS, HD),
        ],
        axis=-2,
    )

    def send_far(window_grad):
        count = lax.axis_size("blk") * tok_dev
        row_limit = count * 2 * HEADS
        inside = (flat_index >= 0) & (flat_index < row_limit)
        safe_index = jnp.where(inside, flat_index, row_limit)
        table = jnp.zeros((row_limit, HD), jnp.float32).at[safe_index].add(window_grad, mode="drop")
        return lax.psum_scatter(
            table.reshape(count, 2 * model_width), "blk", scatter_dimension=0, tiled=True
        )

    far_back = lax.map(send_far, grad_far)
    here_kv = jnp.stack([grad_key_here, grad_value_here], axis=2).reshape(
        windows, tok_dev, 2 * model_width
    )
    grad_kv = grad_ext[:, BS : BS + tok_dev] + far_back + here_kv
    grad_kv = (
        grad_kv.at[:, :BS].add(rim_back[:, :BS]).at[:, tok_dev - BS :].add(rim_back[:, 3 * BS :])
    )
    sum_query = summed[..., :model_width]
    sum_kv = summed[..., model_width:]
    grad_kv = (
        grad_kv.at[:, :BS]
        .add(jnp.where(is_first, sum_kv[:, 0], 0.0))
        .at[:, tok_dev - BS :]
        .add(jnp.where(is_final, sum_kv[:, 1], 0.0))
    )
    grad_q = grad_query.reshape(windows, tok_dev, model_width)
    grad_q = (
        grad_q.at[:, :BS]
        .add(jnp.where(is_first, sum_query[:, 0], 0.0))
        .at[:, tok_dev - BS :]
        .add(jnp.where(is_final, sum_query[:, 1], 0.0))
    )
    qkv_low = (
        jnp.concatenate([grad_q, grad_kv], axis=-1)
        .astype(jnp.bfloat16)
        .reshape(row_count, 3 * model_width)
    )
    grad_qkv = jnp.einsum("rd,re->de", normed_low, qkv_low, preferred_element_type=jnp.float32)
    grad_bias_q = jnp.sum(qkv_low[:, :model_width].astype(jnp.float32), axis=0)
    grad_bias_v = jnp.sum(qkv_low[:, 2 * model_width :].astype(jnp.float32), axis=0)
    grad_normed = jnp.einsum(
        "re,de->rd", qkv_low, w_qkv, preferred_element_type=jnp.float32
    ).reshape(windows, tok_dev, model_width)
    grad_start, grad_gain_one, grad_shift_one = norm_one_back(grad_normed)
    input_grad = (grad_resid + grad_start).astype(jnp.bfloat16)
    grad_list = (
        grad_qkv,
        grad_bias_q,
        grad_bias_v,
        grad_out,
        grad_bias_out,
        grad_gain_one,
        grad_shift_one,
        grad_gain_two,
        grad_shift_two,
        grad_in,
        grad_bias_in,
        grad_down,
        grad_bias_down,
    )
    return (result, input_grad, grad_list)


def per_device(
    inputs,
    species,
    random_blocks,
    qkv_weight,
    q_bias,
    v_bias,
    out_weight,
    out_bias,
    norm1_gain,
    norm1_bias,
    norm2_gain,
    norm2_bias,
    ffn_in_weight,
    ffn_in_bias,
    ffn_out_weight,
    ffn_out_bias,
    cotangent,
):
    weights = (
        qkv_weight,
        q_bias,
        v_bias,
        out_weight,
        out_bias,
        norm1_gain,
        norm1_bias,
        norm2_gain,
        norm2_bias,
        ffn_in_weight,
        ffn_in_bias,
        ffn_out_weight,
        ffn_out_bias,
    )
    groups = lax.axis_size("win")
    group_index = lax.axis_index("win")
    slot_rank = rank_within(species)
    local_count = inputs.shape[0]
    slot_count = cotangent.shape[0]
    members = jnp.sum((species == group_index).astype(jnp.int32))
    outgoing = group_buffer(inputs, species, slot_rank, group_index, groups, slot_count)
    arrived = lax.all_to_all(outgoing, "win", split_axis=0, concat_axis=0, tiled=True)
    tokens = jnp.sum(arrived.astype(jnp.float32), axis=0).astype(jnp.bfloat16)
    live_slots = jnp.arange(slot_count, dtype=jnp.int32) < members
    result, slot_grad, grad_list = layer_pass(tokens, cotangent, live_slots, random_blocks, weights)
    back_buffer = anchor_buffer(slot_grad, species, slot_rank, group_index, groups, local_count)
    returned = lax.all_to_all(back_buffer, "win", split_axis=0, concat_axis=0, tiled=True)
    input_grad = jnp.sum(returned.astype(jnp.float32), axis=0).astype(jnp.bfloat16)
    summed_grads = lax.psum(
        (
            grad_list[0],
            grad_list[1],
            grad_list[2],
            grad_list[3],
            grad_list[4],
            grad_list[5],
            grad_list[6],
            grad_list[7],
            grad_list[8],
            grad_list[9],
            grad_list[10],
            grad_list[11],
            grad_list[12],
        ),
        ("win", "blk"),
    )
    return (result, input_grad) + tuple(summed_grads)


def solution(mesh):
    in_specs = (
        P("win", "blk", None),
        P(),
        P(),
        P(),
        P(),
        P(),
        P(),
        P(),
        P(),
        P(),
        P(),
        P(),
        P(),
        P(),
        P(),
        P(),
        P("win", "blk", None),
    )
    out_specs = (
        P("win", "blk", None),
        P("win", "blk", None),
        P(),
        P(),
        P(),
        P(),
        P(),
        P(),
        P(),
        P(),
        P(),
        P(),
        P(),
        P(),
        P(),
    )
    return jax.shard_map(
        per_device, mesh=mesh, in_specs=in_specs, out_specs=out_specs, check_vma=False
    )
```

profile of v0, /device:TPU:0, one launch (start us, length us, event | category | flops | bytes accessed | tf_op | source)
XLA Modules:
  0.0 2594.4 jit_solution(9096798219865174287)
XLA Ops:
  32.2 24.7 all-to-all-done
  85.0 100.5 %all-reduce.16 = bf16[4,2,64,2304]{3,2,0,1:T(8,128)(2,1)} all-reduce(f32[4,2,64,2304]{3,2,0,1:T(8,128)} %maximum_convert_fusion), channel_id=1, replica_groups=mesh['win'=4,'blk'=8] {'blk'}, use_global_device_ids=true, to_apply=%region_5.6 | all-reduce | flops 1179648 | bytes 7077888 | tf_op jit(solution)/shard_map/psum | solution.py:162
  199.0 14.5 all-gather.1
  214.2 14.5 all-gather.2
  229.5 16.6 while.50
  247.7 8.5 fusion.68
  287.8 386.0 %while.51 = (s32[]{:T(128)}, bf16[4,2,12,3,64,2,64]{6,5,4,3,2,1,0:T(2,128)(2,1)}, bf16[4,128,1536]{2,1,0:T(8,128)(2,1)}, s32[2,12,3,64]{3,1,2,0:T(8,128)}, s32[]{:T(128)}) while((s32[]{:T(128)}, bf16[4,2,12,3,64,2,64]{6,5,4,3,2,1,0:T(2,128)(2,1)}, bf16[4,128,1536]{2,1,0:T(8,128)(2,1)}, s32[2,12,3,64]{3,1,2,0:T(8,128)}, ...), condition=%wide.region_7.8_spmd.clone, body=%wide.region_6.7_spmd.clone.sunk | while | flops 737282 | bytes 25721972 | solution.py:182
  303.1 25.4 all-gather.8.cloned.1.call-done
  328.6 8.9 reshape.911
  337.4 38.2 %gather_fusion = bf16[9216,64]{1,0:T(8,128)(2,1)} fusion(bf16[24576,64]{1,0:T(8,128)(2,1)} %reshape.911, s32[9216]{0:T(1024)} %broadcast_clamp_fusion.2), kind=kCustom, calls=%fused_computation.clone.clone.1 | custom fusion | bytes 2396160 | tf_op jit(solution)/shard_map/while/body/eval_jaxpr/jit(_take)/gather | solution.py:180
  375.6 9.1 fusion.225
  399.8 25.2 all-gather.8.cloned.1.call-done
  425.0 8.9 reshape.911
  433.9 38.2 %gather_fusion = bf16[9216,64]{1,0:T(8,128)(2,1)} fusion(bf16[24576,64]{1,0:T(8,128)(2,1)} %reshape.911, s32[9216]{0:T(1024)} %broadcast_clamp_fusion.2), kind=kCustom, calls=%fused_computation.clone.clone.1 | custom fusion | bytes 2396160 | tf_op jit(solution)/shard_map/while/body/eval_jaxpr/jit(_take)/gather | solution.py:180
  472.0 9.1 fusion.225
  496.3 25.2 all-gather.8.cloned.1.call-done
  521.5 8.9 reshape.911
  530.4 38.2 %gather_fusion = bf16[9216,64]{1,0:T(8,128)(2,1)} fusion(bf16[24576,64]{1,0:T(8,128)(2,1)} %reshape.911, s32[9216]{0:T(1024)} %broadcast_clamp_fusion.2), kind=kCustom, calls=%fused_computation.clone.clone.1 | custom fusion | bytes 2396160 | tf_op jit(solution)/shard_map/while/body/eval_jaxpr/jit(_take)/gather | solution.py:180
  568.5 9.1 fusion.225
  592.8 24.9 all-gather.8.cloned.1.call-done
  617.7 8.9 reshape.911
  626.5 38.2 %gather_fusion = bf16[9216,64]{1,0:T(8,128)(2,1)} fusion(bf16[24576,64]{1,0:T(8,128)(2,1)} %reshape.911, s32[9216]{0:T(1024)} %broadcast_clamp_fusion.2), kind=kCustom, calls=%fused_computation.clone.clone.1 | custom fusion | bytes 2396160 | tf_op jit(solution)/shard_map/while/body/eval_jaxpr/jit(_take)/gather | solution.py:180
  664.7 9.1 fusion.225
  674.4 116.1 %all-reduce.17 = bf16[4,2,64,12,64]{2,4,1,3,0:T(8,128)(2,1)} all-reduce(f32[4,2,64,12,64]{2,4,1,3,0:T(8,128)} %convolution_bitcast_fusion.2), channel_id=1, replica_groups=mesh['win'=4,'blk'=8] {'blk'}, use_global_device_ids=true, to_apply=%region_14.15 | all-reduce | flops 393216 | bytes 2359296 | tf_op jit(solution)/shard_map/psum | solution.py:229
  790.5 22.8 fusion.179
  813.3 7.2 copy.386
  840.7 10.2 reshape.808
  850.8 13.6 slice_bitcast_fusion.8
  864.4 41.9 %pad_maximum_fusion.3 = bf16[4,2,3,64,2,12,64]{3,1,6,5,4,0,2:T(2,128)(2,1)} fusion(bf16[4,2,1,64,2,12,64]{3,1,6,5,4,0,2:T(2,128)(2,1)S(1)} %get-tuple-element.458, bf16[4,2,1,64,2,12,64]{3,1,6,5,4,0,2:T(2,128)(2,1)S(1)} %get-tuple-element.459, bf16[4,2,1,64,2,12,64]{3,1,6,5,4,0,2:T(2,128)(2,1)S(1)} %get-tuple-element.457), kind=kLoop, calls=%fused_computation.45 | loop fusion | flops 4718592 | bytes 9437184 | tf_op jit(solution)/shard_map/stack | solution.py:168
  906.3 21.7 copy.288
  934.1 10.2 fusion.172
  944.4 7.5 exponential_reduce_fusion
  952.6 8.2 fusion.19
  983.7 9.5 scatter.6
  995.7 11.2 scatter.9
  1017.9 19.2 convert_reduce_fusion
  1055.0 8.8 fusion.108
  1076.2 80.8 %multiply_convert_fusion = bf16[4,2,12,64,512]{4,3,2,1,0:T(8,128)(2,1)} fusion(f32[4,2,12,64,192]{4,3,2,1,0:T(8,128)} %fusion.108, f32[4,2,12,64,128]{4,3,2,1,0:T(8,128)} %convolution_bitcast_fusion.1, f32[4,2,12,64,192]{4,3,2,1,0:T(8,128)} %fusion.29, f32[4,2,12,64]{3,2,1,0:T(8,128)} %copy-done.60, f32[4,2,12,64,192]{4,3,2,1,0:T(8,128)} %fusion.114, ...), kind=kOutput, calls=%fused_computation.39 | output fusion | flops 56629760 | bytes 31482880 | tf_op jit(solution)/shard_map/sub | solution.py:308
  1157.0 6.9 fusion.31
  1224.5 71.6 %all-reduce.18 = (bf16[4,2,64,12,64]{4,2,1,3,0:T(8,128)(2,1)}, f32[4,2,12,64]{3,2,0,1:T(8,128)}) all-reduce(f32[4,2,64,12,64]{4,2,1,3,0:T(8,128)} %pad_maximum_fusion.7, f32[4,2,12,64]{3,2,0,1:T(8,128)} %maximum_bitcast_fusion), channel_id=1, replica_groups=mesh['win'=4,'blk'=8] {'blk'}, use_global_device_ids=true, to_apply=%region_20.21 | all-reduce | flops 399360 | bytes 2408448 | tf_op jit(solution)/shard_map/psum | solution.py:282
  1340.3 8.6 copy.345
  1348.9 14.4 pad_maximum_fusion
  1365.9 613.5 %while.52 = (s32[]{:T(128)}, f32[4,128,1536]{2,1,0:T(8,128)}, f32[4,2,12,3,64,2,64]{6,4,3,2,1,0,5:T(8,128)}, s32[2,12,3,64]{3,2,1,0:T(4,128)}, s32[]{:T(128)}, /*index=5*/f32[]{:T(128)}) while((s32[]{:T(128)}, f32[4,128,1536]{2,1,0:T(8,128)}, f32[4,2,12,3,64,2,64]{6,4,3,2,1,0,5:T(8,128)}, s32[2,12,3,64]{3,2,1,0:T(4,128)}, ...), condition=%wide.region_29.30_spmd.clone, body=%wide.region_26.29_spmd.clone.sunk | while | flops 681986 | bytes 51247740 | solution.py:418
  1382.8 55.0 %scatter_custom_fusion.6 = f32[24576,64]{1,0:T(8,128)} fusion(s32[9216]{0:T(1024)} %reshape.915, f32[9216,64]{1,0:T(8,128)} %bitcast.375, f32[]{:T(128)} %constant.404.clone.1..sunk), kind=kCustom, calls=%fused_computation.24.clone.1 | custom fusion | flops 589824 | bytes 6291968 | tf_op jit(solution)/shard_map/while/body/eval_jaxpr/scatter-add | solution.py:413
  1437.8 11.1 reshape.916
  1448.9 69.4 %reduce-scatter.2.cloned.1.call-done = f32[128,1536]{1,0:T(8,128)} async-done(((f32[1024,1536]{1,0:T(8,128)}), f32[128,1536]{1,0:T(8,128)}) %reduce-scatter.2.cloned.1.call-update) | async-done | bytes 786448 | tf_op jit(solution)/shard_map/while/body/eval_jaxpr/reduce_scatter | solution.py:414
  1536.8 55.0 %scatter_custom_fusion.6 = f32[24576,64]{1,0:T(8,128)} fusion(s32[9216]{0:T(1024)} %reshape.915, f32[9216,64]{1,0:T(8,128)} %bitcast.375, f32[]{:T(128)} %constant.404.clone.1..sunk), kind=kCustom, calls=%fused_computation.24.clone.1 | custom fusion | flops 589824 | bytes 6291968 | tf_op jit(solution)/shard_map/while/body/eval_jaxpr/scatter-add | solution.py:413
  1591.9 11.1 reshape.916
  1603.0 68.3 %reduce-scatter.2.cloned.1.call-done = f32[128,1536]{1,0:T(8,128)} async-done(((f32[1024,1536]{1,0:T(8,128)}), f32[128,1536]{1,0:T(8,128)}) %reduce-scatter.2.cloned.1.call-update) | async-done | bytes 786448 | tf_op jit(solution)/shard_map/while/body/eval_jaxpr/reduce_scatter | solution.py:414
  1689.8 55.0 %scatter_custom_fusion.6 = f32[24576,64]{1,0:T(8,128)} fusion(s32[9216]{0:T(1024)} %reshape.915, f32[9216,64]{1,0:T(8,128)} %bitcast.375, f32[]{:T(128)} %constant.404.clone.1..sunk), kind=kCustom, calls=%fused_computation.24.clone.1 | custom fusion | flops 589824 | bytes 6291968 | tf_op jit(solution)/shard_map/while/body/eval_jaxpr/scatter-add | solution.py:413
  1744.8 11.1 reshape.916
  1756.0 68.3 %reduce-scatter.2.cloned.1.call-done = f32[128,1536]{1,0:T(8,128)} async-done(((f32[1024,1536]{1,0:T(8,128)}), f32[128,1536]{1,0:T(8,128)}) %reduce-scatter.2.cloned.1.call-update) | async-done | bytes 786448 | tf_op jit(solution)/shard_map/while/body/eval_jaxpr/reduce_scatter | solution.py:414
  1842.8 55.0 %scatter_custom_fusion.6 = f32[24576,64]{1,0:T(8,128)} fusion(s32[9216]{0:T(1024)} %reshape.915, f32[9216,64]{1,0:T(8,128)} %bitcast.375, f32[]{:T(128)} %constant.404.clone.1..sunk), kind=kCustom, calls=%fused_computation.24.clone.1 | custom fusion | flops 589824 | bytes 6291968 | tf_op jit(solution)/shard_map/while/body/eval_jaxpr/scatter-add | solution.py:413
  1897.8 11.1 reshape.916
  1908.9 68.3 %reduce-scatter.2.cloned.1.call-done = f32[128,1536]{1,0:T(8,128)} async-done(((f32[1024,1536]{1,0:T(8,128)}), f32[128,1536]{1,0:T(8,128)}) %reduce-scatter.2.cloned.1.call-update) | async-done | bytes 786448 | tf_op jit(solution)/shard_map/while/body/eval_jaxpr/reduce_scatter | solution.py:414
  1980.2 8.5 fusion.183
  1988.7 11.7 pad_maximum_fusion.2
  2000.4 21.5 copy.343
  2021.9 19.5 reshape.828
  2083.6 6.6 fusion.37
  2149.4 64.0 %all-reduce.1 = (f32[768]{0:T(1024)}, f32[768]{0:T(1024)}, f32[768]{0:T(1024)}, f32[768]{0:T(1024)}, f32[768]{0:T(1024)}, /*index=5*/f32[768]{0:T(1024)}, f32[768]{0:T(1024)}, f32[3072]{0:T(1024)}, f32[768]{0:T(1024)}) all-reduce(f32[768]{0:T(1024)S(1)} %get-tuple-element.444, ...), channel_id=1, replica_groups=mesh['win'=4,'blk'=8] {'win','blk'}, use_global_device_ids=true, to_apply=%region_35.36 | all-reduce | flops 9216 | bytes 73728 | tf_op jit(solution)/shard_map/psum | solution.py:520
  2215.9 349.6 %all-reduce.15.cloned.1.call-done = (f32[768,2304]{1,0:T(8,128)}, f32[768,768]{1,0:T(8,128)}, f32[768,3072]{1,0:T(8,128)}, f32[3072,768]{1,0:T(8,128)}) async-done(((f32[768,2304]{1,0:T(8,128)}, f32[768,768]{1,0:T(8,128)}, f32[768,3072]{1,0:T(8,128)}, f32[3072,768]{1,0:T(8,128)}), (f32[768,2304]{1,0:T(8,128)}, f32[768,768]{1,0:T(8,128)}, f32[768,3072]{1,0:T(8,128)}, ...) | async-done | bytes 28311568 | tf_op jit(solution)/shard_map/psum | solution.py:520
  2565.5 6.6 copy.533
  2573.4 9.3 copy.535
  (515 shorter events, 562.3 us)
Async XLA Ops:
  8.0 56.9 %copy-start = (bf16[768,2304]{1,0:T(8,128)(2,1)S(1)}, bf16[768,2304]{1,0:T(8,128)(2,1)}, u32[]{:S(2)}) copy-start(bf16[768,2304]{1,0:T(8,128)(2,1)} %param.48) | copy-start | bytes 10616836
  14.6 42.3 %all-to-all-start = ((bf16[4,4,128,768]{3,1,2,0:T(4,128)(2,1)}), bf16[4,4,128,768]{3,1,2,0:T(4,128)(2,1)}, u32[]{:S(2)}, u32[]{:S(2)}) async-start(bf16[4,4,128,768]{3,1,2,0:T(4,128)(2,1)} %convolution_convert_fusion), calls=%async_computation.1 | async-start | bytes 6291456 | tf_op jit(solution)/shard_map/all_to_all | solution.py:513
  32.2 32.7 %copy-start.61 = (f32[768]{0:T(1024)S(1)}, f32[768]{0:T(1024)}, u32[]{:S(2)}) copy-start(f32[768]{0:T(1024)} %param.53) | copy-start | bytes 9220
  32.2 32.7 %copy-start.68 = (f32[768]{0:T(1024)S(1)}, f32[768]{0:T(1024)}, u32[]{:S(2)}) copy-start(f32[768]{0:T(1024)} %param.54) | copy-start | bytes 9220
  213.5 15.9 copy-start.57
  265.5 567.6 %collective-permute-start = (bf16[4,64,1536]{2,1,0:T(8,128)(2,1)}, bf16[4,64,1536]{2,1,0:T(8,128)(2,1)}, u32[]{:S(2)}, u32[]{:S(2)}) collective-permute-start(bf16[4,64,1536]{2,1,0:T(8,128)(2,1)} %get-tuple-element.471), channel_id=1, source_target_pairs={{0,1},{1,2},{2,3},{3,4},{4,5},{5,6},{6,7},{8,9},{9,10},{10,11},{11... | collective-permute-start | bytes 2359304 | tf_op jit(solution)/shard_map/ppermute | solution.py:22
  268.7 564.4 %collective-permute-start.1 = (bf16[4,64,1536]{2,1,0:T(8,128)(2,1)}, bf16[4,64,1536]{2,1,0:T(8,128)(2,1)}, u32[]{:S(2)}, u32[]{:S(2)}) collective-permute-start(bf16[4,64,1536]{2,1,0:T(8,128)(2,1)} %get-tuple-element.472), channel_id=1, source_target_pairs={{1,0},{2,1},{3,2},{4,3},{5,4},{6,5},{7,6},{9,8},{10,9},{11,10},{12... | collective-permute-start | bytes 2359304 | tf_op jit(solution)/shard_map/ppermute | solution.py:25
  287.8 40.7 %all-gather.8.cloned.1.call-start = ((), (), s32[]{:S(2)}) async-start(), calls=%async_computation.6 | async-start | bytes 3538944 | tf_op jit(solution)/shard_map/while/body/eval_jaxpr/all_gather | solution.py:179
  384.7 40.3 %all-gather.8.cloned.1.call-start = ((), (), s32[]{:S(2)}) async-start(), calls=%async_computation.6 | async-start | bytes 3538944 | tf_op jit(solution)/shard_map/while/body/eval_jaxpr/all_gather | solution.py:179
  481.2 40.3 %all-gather.8.cloned.1.call-start = ((), (), s32[]{:S(2)}) async-start(), calls=%async_computation.6 | async-start | bytes 3538944 | tf_op jit(solution)/shard_map/while/body/eval_jaxpr/all_gather | solution.py:179
  577.6 40.0 %all-gather.8.cloned.1.call-start = ((), (), s32[]{:S(2)}) async-start(), calls=%async_computation.6 | async-start | bytes 3538944 | tf_op jit(solution)/shard_map/while/body/eval_jaxpr/all_gather | solution.py:179
  673.8 535.6 %all-reduce.11.cloned.1.call-start = ((), (), s32[]{:S(2)}) async-start(), calls=%async_computation.3 | async-start | bytes 6291456 | tf_op jit(solution)/shard_map/psum | solution.py:229
  928.0 6.1 copy-start.13
  928.0 6.1 copy-start.74
  928.0 16.3 slice-start.6
  934.1 17.8 copy-start.3
  934.1 10.2 slice-start.7
  944.3 16.4 slice-start
  944.4 16.4 slice-start.1
  952.6 8.2 slice-start.2
  993.1 16.0 copy-start.92
  1009.2 8.7 slice-start.19
  1011.9 28.1 %copy-start.25 = (f32[512,768]{1,0:T(8,128)}, f32[512,768]{1,0:T(8,128)S(1)}, u32[]{:S(2)}) copy-start(f32[512,768]{1,0:T(8,128)S(1)} %get-tuple-element.449) | copy-start | bytes 4718596
  1011.9 29.5 %copy-start.29 = (f32[512,768]{1,0:T(8,128)}, f32[512,768]{1,0:T(8,128)S(1)}, u32[]{:S(2)}) copy-start(f32[512,768]{1,0:T(8,128)S(1)} %get-tuple-element.479) | copy-start | bytes 4718596
  1012.0 29.5 %copy-start.77 = (f32[4,128]{1,0:T(4,128)}, f32[4,128]{1,0:T(4,128)S(1)}, u32[]{:S(2)}) copy-start(f32[4,128]{1,0:T(4,128)S(1)} %get-tuple-element.477) | copy-start | bytes 6148
  1012.3 24.8 slice-start.17
  1017.9 19.3 copy-start.45
  1017.9 19.3 slice-start.18
  1055.0 15.4 copy-start.6
  1055.0 15.4 slice-start.3
  1055.0 15.4 slice-start.4
  1063.8 6.6 slice-start.5
  1157.0 6.9 copy-start.14
  1163.8 6.5 copy-start.9
  1172.5 7.6 slice-start.8
  1180.1 10.2 slice-start.13
  1180.1 10.2 slice-start.15
  1196.7 7.1 copy-start.99
  1348.9 14.4 copy-start.41
  1348.9 14.4 copy-start.42
  1348.9 14.4 copy-start.43
  1366.3 152.1 %reduce-scatter.2.cloned.1.call-start = ((), (), s32[]{:S(2)}) async-start(), calls=%async_computation.7 | async-start | bytes 7077888 | tf_op jit(solution)/shard_map/while/body/eval_jaxpr/reduce_scatter | solution.py:414
  1520.4 150.9 %reduce-scatter.2.cloned.1.call-start = ((), (), s32[]{:S(2)}) async-start(), calls=%async_computation.7 | async-start | bytes 7077888 | tf_op jit(solution)/shard_map/while/body/eval_jaxpr/reduce_scatter | solution.py:414
  1673.4 150.9 %reduce-scatter.2.cloned.1.call-start = ((), (), s32[]{:S(2)}) async-start(), calls=%async_computation.7 | async-start | bytes 7077888 | tf_op jit(solution)/shard_map/while/body/eval_jaxpr/reduce_scatter | solution.py:414
  1826.4 150.9 %reduce-scatter.2.cloned.1.call-start = ((), (), s32[]{:S(2)}) async-start(), calls=%async_computation.7 | async-start | bytes 7077888 | tf_op jit(solution)/shard_map/while/body/eval_jaxpr/reduce_scatter | solution.py:414
  1979.4 122.5 %all-reduce.13.cloned.1.call-start = ((), (), s32[]{:S(2)}) async-start(), calls=%async_computation.4 | async-start | bytes 9437184 | tf_op jit(solution)/shard_map/psum | solution.py:390
  1980.0 585.5 %all-reduce.15.cloned.1.call-start = ((), (), s32[]{:S(2)}) async-start(), calls=%async_computation.5 | async-start | bytes 56623104 | tf_op jit(solution)/shard_map/psum | solution.py:520
  2047.2 11.5 copy-start.35
  2048.3 10.5 copy-start.21
  2048.3 10.5 copy-start.22
  2053.0 11.1 copy-start.20
  2053.0 11.1 copy-start.52
  2053.0 40.5 %collective-permute-start.3 = (f32[4,64,1536]{2,1,0:T(8,128)}, f32[4,64,1536]{2,1,0:T(8,128)}, u32[]{:S(2)}, u32[]{:S(2)}) collective-permute-start(f32[4,64,1536]{2,1,0:T(8,128)} %slice.503), channel_id=1, source_target_pairs={{1,0},{2,1},{3,2},{4,3},{5,4},{6,5},{7,6},{9,8},{10,9},{11,10},{12... | collective-permute-start | bytes 4718600 | tf_op jit(solution)/shard_map/ppermute | solution.py:25
  2054.5 35.7 %collective-permute-start.2 = (f32[4,64,1536]{2,1,0:T(8,128)}, f32[4,64,1536]{2,1,0:T(8,128)}, u32[]{:S(2)}, u32[]{:S(2)}) collective-permute-start(f32[4,64,1536]{2,1,0:T(8,128)} %slice.501), channel_id=1, source_target_pairs={{0,1},{1,2},{2,3},{3,4},{4,5},{5,6},{6,7},{8,9},{9,10},{10,11},{11... | collective-permute-start | bytes 4718600 | tf_op jit(solution)/shard_map/ppermute | solution.py:22
  2101.9 6.4 copy-start.47
  2108.4 8.0 copy-start.48
  2141.6 7.7 copy-start.85
  2141.7 7.7 copy-start.86
  2141.7 7.7 copy-start.87
  2143.1 70.3 %all-to-all-start.1 = ((bf16[4,2,128,768]{3,2,1,0:T(8,128)(2,1)}), bf16[4,2,128,768]{3,2,1,0:T(8,128)(2,1)}, u32[]{:S(2)}, u32[]{:S(2)}) async-start(bf16[4,2,128,768]{3,2,1,0:T(8,128)(2,1)} %copy.354), calls=%async_computation.2 | async-start | bytes 3145728 | tf_op jit(solution)/shard_map/all_to_all | solution.py:518
  2565.4 6.6 copy-start.54
  2572.0 10.7 slice-start.10
  2573.4 9.3 slice-start.11
  2573.4 9.3 slice-start.12
  (76 other events, 258.4 us)
Sparse Core Ops, SparseCore 0:
  290.9 37.5 all-gather.7
  387.8 37.1 all-gather.7
  484.3 37.1 all-gather.7
  580.5 37.1 all-gather.7
  1449.1 69.2 reduce-scatter.1
  1603.1 68.1 reduce-scatter.1
  1756.1 68.1 reduce-scatter.1
  1909.1 68.1 reduce-scatter.1
Sparse Core Ops, SparseCore 1:
  676.6 122.7 all-reduce.10
  1982.2 119.7 all-reduce.12
  2122.9 442.5 all-reduce.14
where the time goes:
time: 2610 us; the launch traced here: 2590 us
  waiting for transfers between devices  756 us (29%)
  local copies, waits for them, and re-layouts  660 us (25%)
  other arithmetic  574 us (22%)
  blocking collectives  381 us (15%)
  matrix products  185 us (7%)
    psum x1, waiting for transfers between devices, per_device(): lax.psum((grad_list[0], grad_list[1], grad_list[2], grad_list[3], grad_li...  350 us
    reduce_scatter x4, waiting for transfers between devices, send_far(): lax.psum_scatter(table.reshape(count, 2 * model_width), 'blk', scatter_di...  274 us
    scatter-add x4, other arithmetic, send_far(): jnp.zeros((row_limit, HD), jnp.float32).at[safe_index]  220 us
    gather x4, local copies, waits for them, and re-layouts, fetch_far(): return jnp.take(whole_kv.reshape(-1, HD), flat_index, axis=0)  153 us
    psum x1, blocking collectives, layer_pass(): end_out, end_exact = lax.psum((part_out, part_exact), 'blk')  116 us
    all_gather x4, waiting for transfers between devices, fetch_far(): whole_kv = lax.all_gather(window_kv, 'blk', axis=0, tiled=True)  101 us
    psum x1, blocking collectives, layer_pass(): shared = lax.psum(end_rows.astype(jnp.float32), 'blk').astype(jnp.bfloat16)  101 us
    sub x1, other arithmetic, layer_pass(): grad_scores = (probs * (grad_probs - row_delta)).astype(jnp.bfloat16)  80.8 us
  transfers between devices with their start and end apart: 17, of which 11 were waited for; matrix products, arithmetic and copies ran while one was open for 33% of the time, Pallas kernels for 0%

commit v1 on v0

v1 whole, which is shorter than its diff:
```python
import functools

import jax
import jax.numpy as jnp
from jax import lax
from jax.experimental import pallas as pl
from jax.experimental.pallas import tpu as pltpu
from jax.sharding import PartitionSpec as P

HEADS = 12
HD = 64
BS = 64
PAIRS = HEADS // 2
PW = 2 * HD

EPS = 1e-05
SCALE = 0.125
MASKED = -1e30
BF = jnp.bfloat16
F32 = jnp.float32
BOTH = ("win", "blk")
VMEM_LIMIT = 56 * 1024 * 1024


def dot(a, b, ca=1, cb=0, precision=None):
    return lax.dot_general(
        a, b, (((ca,), (cb,)), ((), ())), precision=precision, preferred_element_type=F32
    )


def params(grid_dims):
    return pltpu.CompilerParams(
        dimension_semantics=("arbitrary",) * grid_dims, vmem_limit_bytes=VMEM_LIMIT
    )


def cost(flops, nbytes, exps=0):
    return pl.CostEstimate(flops=int(flops), bytes_accessed=int(nbytes), transcendentals=int(exps))


def norm_stats(x):
    width = x.shape[-1]
    mean = jnp.sum(x, axis=-1, keepdims=True) * (1.0 / width)
    c = x - mean
    var = jnp.sum(c * c, axis=-1, keepdims=True) * (1.0 / width)
    rstd = lax.rsqrt(var + EPS)
    return c * rstd, rstd


def norm_back(g, xhat, rstd):
    width = g.shape[-1]
    m1 = jnp.sum(g, axis=-1, keepdims=True) * (1.0 / width)
    m2 = jnp.sum(g * xhat, axis=-1, keepdims=True) * (1.0 / width)
    return rstd * (g - m1 - xhat * m2)


def query_kernel(x_ref, gain_ref, shift_ref, w_ref, b_ref, a_ref, q_ref):
    xhat, _ = norm_stats(x_ref[...].astype(F32))
    a = (xhat * gain_ref[...] + shift_ref[...]).astype(BF)
    a_ref[...] = a
    q = (dot(a, w_ref[...]) + b_ref[...]).astype(BF)
    q_ref[...] = (q.astype(F32) * SCALE).astype(BF)


def query_rows(x, gain, shift, w_qkv, b_q):
    rows, d = x.shape
    tile = rows // 2
    row = pl.BlockSpec((tile, d), lambda i: (i, 0))
    vec = pl.BlockSpec((1, d), lambda i: (0, 0))
    return pl.pallas_call(
        query_kernel,
        grid=(rows // tile,),
        in_specs=[row, vec, vec, pl.BlockSpec((d, d), lambda i: (0, 0)), vec],
        out_specs=[row, row],
        out_shape=[jax.ShapeDtypeStruct((rows, d), BF)] * 2,
        compiler_params=params(1),
        cost_estimate=cost(2 * rows * d * d, 2 * d * d + 6 * rows * d),
        name="query_rows",
    )(x, gain, shift, w_qkv, b_q)


def kv_kernel(x_ref, gain_ref, shift_ref, wk_ref, wv_ref, bv_ref, a_ref, k_ref, v_ref):
    xhat, _ = norm_stats(x_ref[...].astype(F32))
    a = (xhat * gain_ref[...] + shift_ref[...]).astype(BF)
    a_ref[...] = a
    k_ref[...] = dot(a, wk_ref[...]).astype(BF)
    v_ref[...] = (dot(a, wv_ref[...]) + bv_ref[...]).astype(BF)


def kv_rows(x, gain, shift, w_qkv, b_v):
    rows, d = x.shape
    tile = min(rows, 512)
    row = pl.BlockSpec((tile, d), lambda i: (i, 0))
    vec = pl.BlockSpec((1, d), lambda i: (0, 0))
    return pl.pallas_call(
        kv_kernel,
        grid=(rows // tile,),
        in_specs=[
            row,
            vec,
            vec,
            pl.BlockSpec((d, d), lambda i: (0, 1)),
            pl.BlockSpec((d, d), lambda i: (0, 2)),
            vec,
        ],
        out_specs=[row, row, row],
        out_shape=[jax.ShapeDtypeStruct((rows, d), BF)] * 3,
        compiler_params=params(1),
        cost_estimate=cost(4 * rows * d * d, 4 * d * d + 8 * rows * d),
        name="kv_rows",
    )(x, gain, shift, w_qkv, w_qkv, b_v)


def head_stack(pair):
    lane = lax.broadcasted_iota(jnp.int32, pair.shape, 1)
    zero = jnp.zeros_like(pair)
    return jnp.concatenate([jnp.where(lane < HD, pair, zero), jnp.where(lane < HD, zero, pair)], axis=0)


def head_select(both):
    rows = both.shape[0] // 2
    lane = lax.broadcasted_iota(jnp.int32, (rows, both.shape[1]), 1)
    return jnp.where(lane < HD, both[:rows], both[rows:])


def biased_scores(k, q2, bias):
    s = dot(k, q2, 1, 1)
    keys, lanes = s.shape
    return (s.reshape(keys // BS, BS, lanes) + bias[:, None, :]).reshape(keys, lanes)


def attend_kernel(q_ref, k_ref, v_ref, bias_ref, o_ref, lse_ref):
    q2 = head_stack(q_ref[...])
    s = biased_scores(k_ref[...], q2, bias_ref[0])
    top = jnp.max(s, axis=0, keepdims=True)
    e = jnp.exp(s - top)
    total = jnp.sum(e, axis=0, keepdims=True)
    p = (e * (1.0 / total)).astype(BF)
    o_t = dot(v_ref[...], p, 0, 0)
    o_ref[...] = head_select(o_t.T).astype(BF)
    lse_ref[0, 0] = top + jnp.log(total)


def attend(q, k, v, bias, windows):
    rows, d = q.shape
    tok = rows // windows
    keys = k.shape[0] // windows
    nkb = keys // BS
    q_spec = pl.BlockSpec((tok, PW), lambda w, p: (w, p))
    k_spec = pl.BlockSpec((keys, PW), lambda w, p: (w, p))
    return pl.pallas_call(
        attend_kernel,
        grid=(windows, PAIRS),
        in_specs=[q_spec, k_spec, k_spec, pl.BlockSpec((1, nkb, 2 * tok), lambda w, p: (p, 0, 0))],
        out_specs=[q_spec, pl.BlockSpec((1, 1, 1, 2 * tok), lambda w, p: (w, p, 0, 0))],
        out_shape=[
            jax.ShapeDtypeStruct((rows, d), BF),
            jax.ShapeDtypeStruct((windows, PAIRS, 1, 2 * tok), F32),
        ],
        compiler_params=params(2),
        cost_estimate=cost(
            4 * windows * PAIRS * keys * 2 * tok * PW, 4 * k.size, windows * PAIRS * keys * 2 * tok
        ),
        name="attend",
    )(q, k, v, bias)


def ffn_kernel(
    x_ref,
    o_ref,
    dy_ref,
    wo_ref,
    bo_ref,
    gain_ref,
    shift_ref,
    wi_ref,
    bi_ref,
    wd_ref,
    bd_ref,
    y_ref,
    dx1_ref,
    do_ref,
    gw_ref,
    gwo_ref,
    gbi_ref,
    vec_ref,
    x1_s,
    h2_s,
    h2t_s,
    y_s,
    dh_s,
):
    step = pl.program_id(0)

    @pl.when(step == 0)
    def _():
        x1 = x_ref[...].astype(F32) + (dot(o_ref[...], wo_ref[...]) + bo_ref[...])
        x1_s[...] = x1
        xhat, _ = norm_stats(x1)
        h2 = xhat * gain_ref[...] + shift_ref[...]
        h2_s[...] = h2.astype(BF)
        h2t_s[...] = h2.T.astype(BF)
        y_s[...] = jnp.zeros_like(y_s)
        dh_s[...] = jnp.zeros_like(dh_s)

    dy = dy_ref[...]
    wi = wi_ref[...]
    wd = wd_ref[...]
    u = dot(h2_s[...], wi) + bi_ref[0]
    half = 0.5 * (1.0 + lax.erf(u * 0.7071067811865476))
    f = (u * half).astype(BF)
    slope = half + u * (jnp.exp(u * u * -0.5) * 0.3989422804014327)
    du = dot(dy, wd, 1, 1) * slope
    du_low = du.astype(BF)
    y_s[...] += dot(f, wd)
    dh_s[...] += dot(du_low, wi, 1, 1)
    gw_ref[0, 0] = dot(f, dy, 0, 0).astype(BF)
    gw_ref[0, 1] = dot(h2t_s[...], du_low).astype(BF)
    gbi_ref[0] = jnp.sum(du_low.astype(F32), axis=0, keepdims=True)

    @pl.when(step == pl.num_programs(0) - 1)
    def _():
        x1 = x1_s[...]
        y_ref[...] = (x1 + (y_s[...] + bd_ref[...])).astype(BF)
        dyf = dy.astype(F32)
        dh = dh_s[...]
        xhat, rstd = norm_stats(x1)
        dx1 = dyf + norm_back(dh * gain_ref[...], xhat, rstd)
        dx1_ref[...] = dx1
        dx1r = dx1.astype(BF)
        do_ref[...] = dot(dx1r, wo_ref[...], 1, 1).astype(BF)
        gwo_ref[...] = dot(o_ref[...], dx1r, 0, 0).astype(BF)
        vec_ref[0:1] = jnp.sum(dyf, axis=0, keepdims=True)
        vec_ref[1:2] = jnp.sum(dh * xhat, axis=0, keepdims=True)
        vec_ref[2:3] = jnp.sum(dh, axis=0, keepdims=True)
        vec_ref[3:4] = jnp.sum(dx1r.astype(F32), axis=0, keepdims=True)
        vec_ref[4:8] = jnp.zeros((4, vec_ref.shape[1]), F32)


def ffn(x, o, dy, w_out, b_out, gain, shift, w_in, b_in, w_down, b_down):
    rows, d = x.shape
    ff = w_in.shape[1]
    steps = ff // d
    row = pl.BlockSpec((rows, d), lambda t: (0, 0))
    vec = pl.BlockSpec((1, d), lambda t: (0, 0))
    square = pl.BlockSpec((d, d), lambda t: (0, 0))
    lane_vec = pl.BlockSpec((1, 1, d), lambda t: (t, 0, 0))
    return pl.pallas_call(
        ffn_kernel,
        grid=(steps,),
        in_specs=[
            row,
            row,
            row,
            square,
            vec,
            vec,
            vec,
            pl.BlockSpec((d, d), lambda t: (0, t)),
            lane_vec,
            pl.BlockSpec((d, d), lambda t: (t, 0)),
            vec,
        ],
        out_specs=[
            row,
            row,
            row,
            pl.BlockSpec((1, 2, d, d), lambda t: (t, 0, 0, 0)),
            square,
            lane_vec,
            pl.BlockSpec((8, d), lambda t: (0, 0)),
        ],
        out_shape=[
            jax.ShapeDtypeStruct((rows, d), BF),
            jax.ShapeDtypeStruct((rows, d), F32),
            jax.ShapeDtypeStruct((rows, d), BF),
            jax.ShapeDtypeStruct((steps, 2, d, d), BF),
            jax.ShapeDtypeStruct((d, d), BF),
            jax.ShapeDtypeStruct((steps, 1, d), F32),
            jax.ShapeDtypeStruct((8, d), F32),
        ],
        scratch_shapes=[
            pltpu.VMEM((rows, d), F32),
            pltpu.VMEM((rows, d), BF),
            pltpu.VMEM((d, rows), BF),
            pltpu.VMEM((rows, d), F32),
            pltpu.VMEM((rows, d), F32),
        ],
        compiler_params=params(1),
        cost_estimate=cost(12 * rows * d * ff + 6 * rows * d * d, 8 * d * ff + 20 * rows * d, 2 * rows * ff),
        name="ffn",
    )(x, o, dy, w_out, b_out, gain, shift, w_in, b_in.reshape(steps, 1, d), w_down, b_down)


def attend_back_kernel(
    q_ref, o_ref, do_ref, k_ref, v_ref, bias_ref, lse_ref, dq_ref, dk_ref, dv_ref, dq_s
):
    step = pl.program_id(2)
    q2 = head_stack(q_ref[...])
    do = do_ref[...]
    do2 = head_stack(do)
    prod = head_stack(do.astype(F32) * o_ref[...].astype(F32))
    delta = dot(jnp.ones((8, PW), F32), prod, 1, 1, lax.Precision.HIGHEST)[0:1]
    k = k_ref[...]
    p = jnp.exp(biased_scores(k, q2, bias_ref[0]) - lse_ref[0, 0])
    dp = dot(v_ref[...], do2, 1, 1)
    ds = (p * (dp - delta)).astype(BF)
    dv_ref[...] = dot(p.astype(BF), do2).astype(BF)
    dk_ref[...] = dot(ds, q2).astype(BF)
    dq_t = dot(k, ds, 0, 0)

    @pl.when(step == 0)
    def _():
        dq_s[...] = dq_t

    @pl.when(step > 0)
    def _():
        dq_s[...] += dq_t

    @pl.when(step == pl.num_programs(2) - 1)
    def _():
        dq_ref[...] = (head_select(dq_s[...].T) * SCALE).astype(BF)


def attend_back(q, o, do, k, v, bias, lse, windows):
    rows, d = q.shape
    tok = rows // windows
    keys = k.shape[0] // windows
    chunk = min(keys, 1024)
    parts = keys // chunk
    nkb = chunk // BS
    q_spec = pl.BlockSpec((tok, PW), lambda w, p, c: (w, p))
    k_spec = pl.BlockSpec((chunk, PW), lambda w, p, c: (w * parts + c, p))
    return pl.pallas_call(
        attend_back_kernel,
        grid=(windows, PAIRS, parts),
        in_specs=[
            q_spec,
            q_spec,
            q_spec,
            k_spec,
            k_spec,
            pl.BlockSpec((1, nkb, 2 * tok), lambda w, p, c: (p, c, 0)),
            pl.BlockSpec((1, 1, 1, 2 * tok), lambda w, p, c: (w, p, 0, 0)),
        ],
        out_specs=[q_spec, k_spec, k_spec],
        out_shape=[
            jax.ShapeDtypeStruct((rows, d), BF),
            jax.ShapeDtypeStruct(k.shape, BF),
            jax.ShapeDtypeStruct(k.shape, BF),
        ],
        scratch_shapes=[pltpu.VMEM((PW, 2 * tok), F32)],
        compiler_params=params(3),
        cost_estimate=cost(
            10 * windows * PAIRS * keys * 2 * tok * PW, 8 * k.size, windows * PAIRS * keys * 2 * tok
        ),
        name="attend_back",
    )(q, o, do, k, v, bias, lse)


def qkv_back_kernel(
    a_ref,
    dk_ref,
    dv_ref,
    al_ref,
    dq_ref,
    wq_ref,
    wk_ref,
    wv_ref,
    da_ref,
    dal_ref,
    gw_ref,
    vec_ref,
    gk_s,
    gv_s,
    vec_s,
):
    step = pl.program_id(0)

    @pl.when(step == 0)
    def _():
        gk_s[...] = jnp.zeros_like(gk_s)
        gv_s[...] = jnp.zeros_like(gv_s)
        al = al_ref[...]
        dq = dq_ref[...]
        dal = dot(dq, wq_ref[...], 1, 1)
        dal_ref[...] = dal
        gw_ref[0] = dot(al, dq, 0, 0).astype(BF)
        vec_s[0:1] = jnp.sum(dal * al.astype(F32), axis=0, keepdims=True)
        vec_s[1:2] = jnp.sum(dal, axis=0, keepdims=True)
        vec_s[2:3] = jnp.sum(dq.astype(F32), axis=0, keepdims=True)
        vec_s[3:8] = jnp.zeros((5, vec_s.shape[1]), F32)

    a = a_ref[...]
    dk = dk_ref[...]
    dv = dv_ref[...]
    da = dot(dk, wk_ref[...], 1, 1) + dot(dv, wv_ref[...], 1, 1)
    da_ref[...] = da.astype(BF)
    a_t = a.T
    gk_s[...] += dot(a_t, dk)
    gv_s[...] += dot(a_t, dv)
    vec_s[0:1] += jnp.sum(da * a.astype(F32), axis=0, keepdims=True)
    vec_s[1:2] += jnp.sum(da, axis=0, keepdims=True)
    vec_s[3:4] += jnp.sum(dv.astype(F32), axis=0, keepdims=True)

    @pl.when(step == pl.num_programs(0) - 1)
    def _():
        gw_ref[1] = gk_s[...].astype(BF)
        gw_ref[2] = gv_s[...].astype(BF)
        vec_ref[...] = vec_s[...]


def qkv_back(a, dk, dv, a_own, dq, w_qkv):
    rows, d = a.shape
    own = dq.shape[0]
    tile = min(rows, 512)
    row = pl.BlockSpec((tile, d), lambda i: (i, 0))
    own_row = pl.BlockSpec((own, d), lambda i: (0, 0))
    return pl.pallas_call(
        qkv_back_kernel,
        grid=(rows // tile,),
        in_specs=[
            row,
            row,
            row,
            own_row,
            own_row,
            pl.BlockSpec((d, d), lambda i: (0, 0)),
            pl.BlockSpec((d, d), lambda i: (0, 1)),
            pl.BlockSpec((d, d), lambda i: (0, 2)),
        ],
        out_specs=[
            row,
            own_row,
            pl.BlockSpec((3, d, d), lambda i: (0, 0, 0)),
            pl.BlockSpec((8, d), lambda i: (0, 0)),
        ],
        out_shape=[
            jax.ShapeDtypeStruct((rows, d), BF),
            jax.ShapeDtypeStruct((own, d), F32),
            jax.ShapeDtypeStruct((3, d, d), BF),
            jax.ShapeDtypeStruct((8, d), F32),
        ],
        scratch_shapes=[pltpu.VMEM((d, d), F32), pltpu.VMEM((d, d), F32), pltpu.VMEM((8, d), F32)],
        compiler_params=params(1),
        cost_estimate=cost(8 * rows * d * d + 4 * own * d * d, 8 * rows * d + 12 * d * d),
        name="qkv_back",
    )(a, dk, dv, a_own, dq, w_qkv, w_qkv, w_qkv)


def input_back_kernel(x_ref, da_ref, dal_ref, dx1_ref, gain_ref, g_ref):
    xhat, rstd = norm_stats(x_ref[...].astype(F32))
    da = da_ref[...].astype(F32) + dal_ref[...]
    g_ref[...] = (dx1_ref[...] + norm_back(da * gain_ref[...], xhat, rstd)).astype(BF)


def input_back(x, da, dal, dx1, gain):
    rows, d = x.shape
    return pl.pallas_call(
        input_back_kernel,
        out_shape=jax.ShapeDtypeStruct((rows, d), BF),
        compiler_params=pltpu.CompilerParams(vmem_limit_bytes=VMEM_LIMIT),
        cost_estimate=cost(20 * rows * d, 14 * rows * d),
        name="input_back",
    )(x, da, dal, dx1, gain)


def swap(x, partner):
    wins, blks = lax.axis_size("win"), lax.axis_size("blk")
    perm = []
    for w in range(wins):
        for b in range(blks):
            pw, pb = partner(w, b)
            perm.append((w * blks + b, pw * blks + pb))
    return lax.ppermute(x, BOTH, perm)


def core_swap(x):
    return swap(x, lambda w, b: (w, b ^ 1))


def chip_swap(x, s):
    return swap(x, lambda w, b: (w, b ^ (2 * s)))


def win_swap(x, s):
    return swap(x, lambda w, b: (w ^ s, b))


def win_turns():
    bits = (lax.axis_size("win") - 1).bit_length()
    even = [1 << i for i in range(bits)]
    return list(zip(even, even[::-1]))


def pick(flag, a, b):
    return jnp.where(flag, a, b)


def add_low(parts):
    total = parts[0].astype(F32)
    for part in parts[1:]:
        total = total + part.astype(F32)
    return total.astype(BF)


def keep_send(x, bit):
    half = x.shape[0] // 2
    low, high = x[:half], x[half:]
    return pick(bit, high, low), pick(bit, low, high)


def scatter_sum(x):
    core = (lax.axis_index("blk") % 2) == 1
    win = lax.axis_index("win")
    chip = lax.axis_index("blk") // 2
    chips = lax.axis_size("blk") // 2
    keep, send = keep_send(x, core)
    x = add_low([keep, core_swap(send)])
    for even, odd in win_turns():
        bit = (win & jnp.where(core, odd, even)) != 0
        keep, send = keep_send(x, bit)
        got = swap(send, lambda w, b: (w ^ (odd if b % 2 else even), b))
        x = add_low([keep, got])
    x = x.reshape((chips, x.shape[0] // chips) + x.shape[1:])
    parts = [lax.dynamic_index_in_dim(x, chip, 0, keepdims=False)]
    for s in range(1, chips):
        parts.append(chip_swap(lax.dynamic_index_in_dim(x, chip ^ s, 0, keepdims=False), s))
    return add_low(parts)


def gather_all(x):
    core = (lax.axis_index("blk") % 2) == 1
    win = lax.axis_index("win")
    chip = lax.axis_index("blk") // 2
    chips = lax.axis_size("blk") // 2
    parts = [x] + [chip_swap(x, s) for s in range(1, chips)]
    out = jnp.zeros((chips,) + x.shape, x.dtype)
    for s, part in enumerate(parts):
        out = lax.dynamic_update_index_in_dim(out, part, chip ^ s, 0)
    x = out.reshape((chips * x.shape[0],) + x.shape[1:])
    for even, odd in win_turns()[::-1]:
        bit = (win & jnp.where(core, odd, even)) != 0
        got = swap(x, lambda w, b: (w ^ (odd if b % 2 else even), b))
        x = jnp.concatenate([pick(bit, got, x), pick(bit, x, got)])
    got = core_swap(x)
    return jnp.concatenate([pick(core, got, x), pick(core, x, got)])


def sum_all(x):
    for s in range((lax.axis_size("blk") - 1).bit_length()):
        x = x + swap(x, lambda w, b: (w, b ^ (1 << s)))
    for s in range((lax.axis_size("win") - 1).bit_length()):
        x = x + win_swap(x, 1 << s)
    return x


def gather_tokens(x):
    blk = lax.axis_index("blk")
    chips = lax.axis_size("blk") // 2
    core, chip = blk % 2, blk // 2
    mine = [x] + [chip_swap(x, s) for s in range(1, chips)]
    theirs = core_swap(jnp.stack(mine, axis=0))
    out = jnp.zeros((x.shape[0], 2 * chips) + x.shape[1:], x.dtype)
    for s in range(chips):
        place = 2 * (chip ^ s)
        out = lax.dynamic_update_index_in_dim(out, mine[s], place + core, 1)
        out = lax.dynamic_update_index_in_dim(out, theirs[s], place + 1 - core, 1)
    return out


def scatter_tokens(x):
    blk = lax.axis_index("blk")
    chips = lax.axis_size("blk") // 2
    core, chip = blk % 2, blk // 2
    x = x.reshape((x.shape[0], chips, 2) + x.shape[2:])
    send = lax.dynamic_index_in_dim(x, 1 - core, 2, keepdims=False)
    keep = lax.dynamic_index_in_dim(x, core, 2, keepdims=False)
    x = add_low([keep, core_swap(send)])
    parts = [lax.dynamic_index_in_dim(x, chip, 1, keepdims=False)]
    for s in range(1, chips):
        parts.append(chip_swap(lax.dynamic_index_in_dim(x, chip ^ s, 1, keepdims=False), s))
    return add_low(parts)


def rank_within(species):
    window = jnp.arange(species.shape[0], dtype=jnp.int32)
    same = species[:, None] == species[None, :]
    earlier = window[None, :] < window[:, None]
    return jnp.sum((same & earlier).astype(jnp.int32), axis=1)


def fetch_cotangent(cot, species, rank, count):
    me = lax.axis_index("win")
    total = None
    for s in range(lax.axis_size("win")):
        rows = []
        for j in range(count):
            w = (me ^ s) * count + j
            row = lax.dynamic_index_in_dim(cot, jnp.minimum(rank[w], cot.shape[0] - 1), 0, keepdims=False)
            rows.append(jnp.where(species[w] == me, row, jnp.zeros((), cot.dtype)))
        part = jnp.stack(rows)
        if s:
            part = win_swap(part, s)
        total = part if total is None else total + part
    return total


def place_result(y, species, rank, slots):
    me = lax.axis_index("win")
    count = y.shape[0]
    wins = lax.axis_size("win")
    parts = jnp.concatenate([y] + [win_swap(y, s) for s in range(1, wins)])
    order = jnp.concatenate([(me ^ s) * count + jnp.arange(count, dtype=jnp.int32) for s in range(wins)])
    here = jnp.where(species[order] == me, rank[order], -1)
    out = []
    for k in range(slots):
        hit = here == k
        row = lax.dynamic_index_in_dim(parts, jnp.argmax(hit), 0, keepdims=False)
        out.append(jnp.where(jnp.any(hit), row, jnp.zeros((), y.dtype)))
    return jnp.stack(out)


def key_bias(random_blocks, tok):
    per = tok // BS
    blk = lax.axis_index("blk")
    total = lax.axis_size("blk") * per
    picks = lax.dynamic_slice_in_dim(random_blocks, blk * per, per, 0)
    i = (blk * per + jnp.arange(per, dtype=jnp.int32))[:, None, None]
    kb = jnp.arange(total, dtype=jnp.int32)[None, None, :]

    def hits(flag):
        return flag.astype(F32)

    m = hits(kb == i - 1) + hits(kb == i) + hits(kb == i + 1)
    m = m + hits((kb == 0) & (i >= 2)) + hits((kb == total - 1) & (i <= total - 3))
    for r in range(picks.shape[2]):
        m = m + hits(picks[:, :, r : r + 1] == kb)
    m = jnp.where((i == 0) | (i == total - 1), 1.0, m)
    bias = jnp.where(m > 0, jnp.log(jnp.maximum(m, 1.0)), MASKED)
    bias = bias.reshape(per, PAIRS, 2, total).transpose(1, 3, 2, 0)
    return jnp.broadcast_to(bias[..., None], bias.shape + (BS,)).reshape(PAIRS, total, 2 * tok)


def per_device(
    inputs,
    species,
    random_blocks,
    qkv_weight,
    q_bias,
    v_bias,
    out_weight,
    out_bias,
    norm1_gain,
    norm1_bias,
    norm2_gain,
    norm2_bias,
    ffn_in_weight,
    ffn_in_bias,
    ffn_out_weight,
    ffn_out_bias,
    cotangent,
):
    count, tok, d = inputs.shape
    rows = count * tok
    blks = lax.axis_size("blk")
    row_vec = lambda v: v.reshape(1, d)
    rank = rank_within(species)

    everything = gather_tokens(inputs).reshape(count * blks * tok, d)
    dy = fetch_cotangent(cotangent, species, rank, count).reshape(rows, d)
    bias = key_bias(random_blocks, tok)
    x = inputs.reshape(rows, d)
    gain1, shift1 = row_vec(norm1_gain), row_vec(norm1_bias)
    a_own, q = query_rows(x, gain1, shift1, qkv_weight, row_vec(q_bias))
    a, k, v = kv_rows(everything, gain1, shift1, qkv_weight, row_vec(v_bias))
    o, lse = attend(q, k, v, bias, count)
    y, dx1, do, g_ffn, g_out, g_bi, vec2 = ffn(
        x,
        o,
        dy,
        out_weight,
        row_vec(out_bias),
        row_vec(norm2_gain),
        row_vec(norm2_bias),
        ffn_in_weight,
        ffn_in_bias,
        ffn_out_weight,
        row_vec(ffn_out_bias),
    )
    result = place_result(y.reshape(count, tok, d), species, rank, cotangent.shape[0])
    steps = g_ffn.shape[0]
    ffn_chunk = scatter_sum(g_ffn.reshape(steps * 2 * d, d))
    dq, dk, dv = attend_back(q, o, do, k, v, bias, lse, count)
    da, da_own, g_qkv, vec1 = qkv_back(a, dk, dv, a_own, dq, qkv_weight)
    da_sum = scatter_tokens(da.reshape(count, blks, tok, d)).reshape(rows, d)
    input_grad = input_back(x, da_sum, da_own, dx1, gain1).reshape(count, tok, d)

    qkvo_chunk = scatter_sum(jnp.concatenate([g_qkv, g_out[None]]).reshape(4 * d, d))
    vecs = sum_all(jnp.concatenate([vec1[:4], vec2[:4], g_bi.reshape(steps, d)]))
    ffn_all = gather_all(ffn_chunk).reshape(steps, 2, d, d)
    qkvo_all = gather_all(qkvo_chunk).reshape(4, d, d)

    ffn_out_grad = ffn_all[:, 0].reshape(steps * d, d).astype(F32)
    ffn_in_grad = ffn_all[:, 1].transpose(1, 0, 2).reshape(d, steps * d).astype(F32)
    qkv_grad = qkvo_all[:3].transpose(1, 0, 2).reshape(d, 3 * d).astype(F32)
    out_grad = qkvo_all[3].astype(F32)
    gain1_grad = (vecs[0] - norm1_bias * vecs[1]) / norm1_gain
    return (
        result,
        input_grad,
        qkv_grad,
        vecs[2],
        vecs[3],
        out_grad,
        vecs[7],
        gain1_grad,
        vecs[1],
        vecs[5],
        vecs[6],
        ffn_in_grad,
        vecs[8:].reshape(steps * d),
        ffn_out_grad,
        vecs[4],
    )


def solution(mesh):
    split = P("win", "blk", None)
    return jax.shard_map(
        per_device,
        mesh=mesh,
        in_specs=(split,) + (P(),) * 15 + (split,),
        out_specs=(split, split) + (P(),) * 13,
        check_vma=False,
    )
```

time: 2610 us -> 480 us (0.18)
  waiting for transfers between devices: 756 us -> 138 us
  local copies, waits for them, and re-layouts: 660 us -> 73 us
  other arithmetic: 574 us -> 100 us
  blocking collectives: 381 us -> 0 us
  matrix products: 185 us -> 0 us
  Pallas kernels: 0 us -> 78.8 us
  starting transfers between devices: 20.7 us -> 61.8 us
    psum x3 -> x0, waiting for transfers between devices: 355 us -> none  [the longest x1 350 us: per_device(): lax.psum((grad_list[0], grad_list[1], grad_list[2], grad_list[3], grad_li...]
    psum x4 -> x0, blocking collectives: 352 us -> none  [the longest x1 116 us: layer_pass(): end_out, end_exact = lax.psum((part_out, part_exact), 'blk')]
    reduce_scatter x4 -> x0, waiting for transfers between devices: 274 us -> none  [send_far(): lax.psum_scatter(table.reshape(count, 2 * model_width), 'blk', scatter_di...]
    scatter-add x12 -> x0, other arithmetic: 239 us -> none  [the longest x4 220 us: send_far(): jnp.zeros((row_limit, HD), jnp.float32).at[safe_index]]
    dot_general x37 -> x0, matrix products: 182 us -> none  [the longest x1 19.2 us: layer_pass(): jnp.einsum('rd,fd->rf', grad_flat, w_down, preferred_element_type=jnp.flo...]
    reshape x25 -> x10, local copies, waits for them, and re-layouts: 173 us -> 9.54 us  [the longest x8 8.09 us: per_device(): row_vec = lambda v: v.reshape(1, d)]
    gather x4 -> x2, local copies, waits for them, and re-layouts: 153 us -> 1.29 us  [place_result(): here = jnp.where(species[order] == me, rank[order], -1)]
    ppermute x4 -> x43, waiting for transfers between devices: 0.01 us -> 138 us  [swap(): return lax.ppermute(x, BOTH, perm)]
  transfers between devices with their start and end apart: 17 -> 43, of which waited for: 11 -> 19; matrix products, arithmetic and copies ran while one was open for 33% -> 21% of each run, Pallas kernels for 0% -> 8%
where the time goes in v1:
time: 480 us; the launch traced here: 472 us
  waiting for transfers between devices  138 us (29%)
  other arithmetic  100 us (21%)
  Pallas kernels  78.8 us (16%)
  local copies, waits for them, and re-layouts  73 us (15%)
  starting transfers between devices  61.8 us (13%)
  between operations  19.7 us (4%)
    ppermute x43, waiting for transfers between devices, swap(): return lax.ppermute(x, BOTH, perm)  138 us
    ppermute x43, starting transfers between devices, swap(): return lax.ppermute(x, BOTH, perm)  61.8 us
    unnamed x60, local copies, waits for them, and re-layouts  38.6 us
    select_n x12, other arithmetic, pick(): return jnp.where(flag, a, b)  24 us
    pallas_call x1, Pallas kernels, qkv_back(): pl.pallas_call(qkv_back_kernel, grid=(rows // tile,), in_specs=[row, row,...  17.9 us
    convert_element_type x8, other arithmetic, add_low(): return total.astype(BF)  17.3 us
    pallas_call x1, Pallas kernels, ffn(): pl.pallas_call(ffn_kernel, grid=(steps,), in_specs=[row, row, row, square...  15.7 us
    pallas_call x1, Pallas kernels, attend_back(): pl.pallas_call(attend_back_kernel, grid=(windows, PAIRS, parts), in_specs...  15.2 us
  transfers between devices with their start and end apart: 43, of which 19 were waited for; matrix products, arithmetic and copies ran while one was open for 21% of the time, Pallas kernels for 8%

profile of v1, /device:TPU:0, one launch (start us, length us, event | category | flops | bytes accessed | tf_op | source)
XLA Modules:
  0.0 471.7 jit_solution(9237602570498910979)
XLA Ops:
  0.6 5.1 %collective-permute-start.2 = (bf16[2,128,768]{2,1,0:T(8,128)(2,1)}, bf16[2,128,768]{2,1,0:T(8,128)(2,1)S(1)}, u32[]{:S(2)}, u32[]{:S(2)}) collective-permute-start(bf16[2,128,768]{2,1,0:T(8,128)(2,1)} %param.17), channel_id=1, source_target_pairs={{0,6},{1,7},{2,4},{3,5},{4,2},{5,3},{6,0},{7,1},{8,14},{9,15},{10,... | collective-permute-start | bytes 1179656 | tf_op jit(solution)/shard_map/ppermute | solution.py:475
  21.9 2.6 collective-permute-start.6
  27.0 12.5 %collective-permute-done.1 = bf16[2,128,768]{2,1,0:T(8,128)(2,1)S(1)} collective-permute-done((bf16[2,128,768]{2,1,0:T(8,128)(2,1)}, bf16[2,128,768]{2,1,0:T(8,128)(2,1)S(1)}, u32[]{:S(2)}, u32[]{:S(2)}) %collective-permute-start.1) | collective-permute-done | bytes 393248 | tf_op jit(solution)/shard_map/ppermute | solution.py:475
  50.8 3.3 query_rows.1
  55.1 2.1 fusion.14
  63.1 9.9 %kv_rows.1 = (bf16[2048,768]{1,0:T(8,128)(2,1)}, bf16[2048,768]{1,0:T(8,128)(2,1)}, bf16[2048,768]{1,0:T(8,128)(2,1)}) custom-call(bf16[2048,768]{1,0:T(8,128)(2,1)} %bitcast.195, f32[1,768]{1,0:T(1,128)} %reshape.451.gain_ref, f32[1,768]{1,0:T(1,128)} %reshape.452.shift_ref, bf16[768,2304]{1,0:T(8,128)(2,1)} %wv_ref.3, bf16[768,2304]{1,0:T(8,128)(2,1)} %wv_ref.3, ...), custom_call_target="tpu_custom_call" | custom-call | flops 4831838208 | bytes 14942208 | tf_op jit(solution)/shard_map/kv_rows/pallas_call | solution.py:95
  73.1 14.0 %attend.1 = (bf16[256,768]{1,0:T(8,128)(2,1)}, f32[2,6,1,256]{3,2,1,0:T(1,128)}) custom-call(bf16[256,768]{1,0:T(8,128)(2,1)} %get-tuple-element.40.q_ref, bf16[2048,768]{1,0:T(8,128)(2,1)} %get-tuple-element.41.k_ref, bf16[2048,768]{1,0:T(8,128)(2,1)} %get-tuple-element.42.v_ref, f32[6,16,256]{2,1,0:T(8,128)} %reshape.456.bias_ref), custom_call_target="tpu_custom_call" | custom-call | flops 1610612736 | bytes 6291456 | tf_op jit(solution)/shard_map/attend/pallas_call | solution.py:151
  87.0 15.7 %ffn.1 = (bf16[256,768]{1,0:T(8,128)(2,1)}, f32[256,768]{1,0:T(8,128)}, bf16[256,768]{1,0:T(8,128)(2,1)}, bf16[4,2,768,768]{3,2,1,0:T(8,128)(2,1)}, bf16[768,768...) custom-call(bf16[256,768]{1,0:T(8,128)(2,1)} %bitcast.189, bf16[256,768]{1,0:T(8,128)(2,1)} %get-tuple-element.43.o_ref, ...), custom_call_target="tpu_custom_call" | custom-call | flops 8153726976 | bytes 22806528 | tf_op jit(solution)/shard_map/ffn/pallas_call | solution.py:248
  102.7 8.3 %broadcast_select_fusion.1 = (bf16[2,2,768,768]{3,2,1,0:T(8,128)(2,1)}, bf16[2,2,768,768]{3,2,1,0:T(8,128)(2,1)}) fusion(pred[]{:T(512)S(6)} %eq.264, bf16[4,2,768,768]{3,2,1,0:T(8,128)(2,1)} %get-tuple-element.64), kind=kLoop, calls=%fused_computation.14 | loop fusion | flops 4718592 | bytes 18874368 | tf_op jit(solution)/shard_map/jit(_where)/select_n | solution.py:497
  111.5 15.2 %attend_back.1 = (bf16[256,768]{1,0:T(8,128)(2,1)}, bf16[2048,768]{1,0:T(8,128)(2,1)}, bf16[2048,768]{1,0:T(8,128)(2,1)}) custom-call(bf16[256,768]{1,0:T(8,128)(2,1)} %get-tuple-element.40.q_ref, bf16[256,768]{1,0:T(8,128)(2,1)} %get-tuple-element.43.o_ref, bf16[256,768]{1,0:T(8,128)(2,1)} %get-tuple-element.50.do_ref, ...), custom_call_target="tpu_custom_call" | custom-call | flops 4026531840 | bytes 12582912 | tf_op jit(solution)/shard_map/attend_back/pallas_call | solution.py:334
  126.7 3.5 fusion
  130.5 1.9 copy-done.1
  133.9 17.9 %qkv_back.1 = (bf16[2048,768]{1,0:T(8,128)(2,1)}, f32[256,768]{1,0:T(8,128)}, bf16[3,768,768]{2,1,0:T(8,128)(2,1)}, f32[8,768]{1,0:T(8,128)}) custom-call(bf16[2048,768]{1,0:T(8,128)(2,1)} %get-tuple-element.49.a_ref, bf16[2048,768]{1,0:T(8,128)(2,1)} %get-tuple-element.52.dk_ref, bf16[2048,768]{1,0:T(8,128)(2,1)} %get-tuple-element.53.dv_ref, ...), custom_call_target="tpu_custom_call" | custom-call | flops 10267656192 | bytes 19660800 | tf_op jit(solution)/shard_map/qkv_back/pallas_call | solution.py:419
  151.8 4.6 broadcast_select_fusion.8
  156.4 5.0 %collective-permute-done.32 = bf16[1536,768]{1,0:T(8,128)(2,1)} collective-permute-done((bf16[1536,768]{1,0:T(8,128)(2,1)S(1)}, bf16[1536,768]{1,0:T(8,128)(2,1)}, u32[]{:S(2)}, u32[]{:S(2)}) %collective-permute-start.32) | collective-permute-done | bytes 2359328 | tf_op jit(solution)/shard_map/ppermute | solution.py:475
  161.3 4.0 add_convert_fusion
  167.8 2.3 fusion.1
  172.7 17.6 %collective-permute-done.33 = bf16[768,768]{1,0:T(8,128)(2,1)} collective-permute-done((bf16[768,768]{1,0:T(8,128)(2,1)S(1)}, bf16[768,768]{1,0:T(8,128)(2,1)}, u32[]{:S(2)}, u32[]{:S(2)}) %collective-permute-start.33) | collective-permute-done | bytes 1179680 | tf_op jit(solution)/shard_map/ppermute | solution.py:475
  190.3 2.4 add_convert_fusion.1
  193.6 2.5 collective-permute-start.36
  196.1 1.9 collective-permute-start.34
  198.0 7.7 %collective-permute-done.36 = bf16[192,768]{1,0:T(8,128)(2,1)} collective-permute-done((bf16[192,768]{1,0:T(8,128)(2,1)}, bf16[192,768]{1,0:T(8,128)(2,1)}, u32[]{:S(2)}, u32[]{:S(2)}) %collective-permute-start.36) | collective-permute-done | bytes 294944 | tf_op jit(solution)/shard_map/ppermute | solution.py:475
  205.7 10.0 %collective-permute-done.35 = bf16[192,768]{1,0:T(8,128)(2,1)} collective-permute-done((bf16[192,768]{1,0:T(8,128)(2,1)}, bf16[192,768]{1,0:T(8,128)(2,1)}, u32[]{:S(2)}, u32[]{:S(2)}) %collective-permute-start.35) | collective-permute-done | bytes 294944 | tf_op jit(solution)/shard_map/ppermute | solution.py:475
  217.2 2.5 collective-permute-start.38
  219.7 1.7 add_convert_fusion.2
  221.4 1.9 collective-permute-start.39
  223.3 7.3 %collective-permute-done.37 = bf16[192,768]{1,0:T(8,128)(2,1)S(1)} collective-permute-done((bf16[192,768]{1,0:T(8,128)(2,1)S(1)}, bf16[192,768]{1,0:T(8,128)(2,1)S(1)}, u32[]{:S(2)}, u32[]{:S(2)}) %collective-permute-start.37) | collective-permute-done | bytes 294944 | tf_op jit(solution)/shard_map/ppermute | solution.py:475
  230.6 8.6 %collective-permute-done.38 = bf16[192,768]{1,0:T(8,128)(2,1)S(1)} collective-permute-done((bf16[192,768]{1,0:T(8,128)(2,1)S(1)}, bf16[192,768]{1,0:T(8,128)(2,1)S(1)}, u32[]{:S(2)}, u32[]{:S(2)}) %collective-permute-start.38) | collective-permute-done | bytes 294944 | tf_op jit(solution)/shard_map/ppermute | solution.py:475
  241.6 20.4 %collective-permute-done.16 = bf16[384,768]{1,0:T(8,128)(2,1)S(1)} collective-permute-done((bf16[384,768]{1,0:T(8,128)(2,1)S(1)}, bf16[384,768]{1,0:T(8,128)(2,1)S(1)}, u32[]{:S(2)}, u32[]{:S(2)}) %collective-permute-start.16) | collective-permute-done | bytes 589856 | tf_op jit(solution)/shard_map/ppermute | solution.py:475
  262.2 2.4 collective-permute-start.19
  264.6 3.8 collective-permute-start.18
  271.9 5.1 %collective-permute-done.18 = bf16[96,768]{1,0:T(8,128)(2,1)S(1)} collective-permute-done((bf16[96,768]{1,0:T(8,128)(2,1)S(1)}, bf16[96,768]{1,0:T(8,128)(2,1)S(1)}, u32[]{:S(2)}, u32[]{:S(2)}) %collective-permute-start.18) | collective-permute-done | bytes 147488 | tf_op jit(solution)/shard_map/ppermute | solution.py:475
  277.3 1.8 collective-permute-start.21
  279.1 2.6 collective-permute-start.22
  281.7 2.3 collective-permute-done.20
  284.0 6.8 %collective-permute-done.21 = bf16[96,768]{1,0:T(8,128)(2,1)S(1)} collective-permute-done((bf16[96,768]{1,0:T(8,128)(2,1)S(1)}, bf16[96,768]{1,0:T(8,128)(2,1)S(1)}, u32[]{:S(2)}, u32[]{:S(2)}) %collective-permute-start.21) | collective-permute-done | bytes 147488 | tf_op jit(solution)/shard_map/ppermute | solution.py:475
  294.4 3.3 constant_dynamic-slice_fusion.3
  303.1 1.8 collective-permute-start.27
  305.8 2.6 broadcast_select_fusion.5
  308.5 2.7 pad_maximum_fusion.1
  311.4 2.5 collective-permute-start.42
  313.9 4.4 collective-permute-done.24
  321.2 4.1 collective-permute-start.28
  327.4 1.8 collective-permute-start.29
  329.8 1.7 collective-permute-done.29
  342.4 1.7 collective-permute-start.9
  351.1 2.3 fusion.2
  354.1 2.3 collective-permute-start.13
  356.5 4.4 collective-permute-done.8
  360.9 2.7 collective-permute-start.12
  365.1 2.6 dynamic-slice_select_fusion.3
  368.7 19.8 %collective-permute-done.12 = bf16[2,128,768]{2,1,0:T(8,128)(2,1)S(1)} collective-permute-done((bf16[2,128,768]{2,1,0:T(8,128)(2,1)S(1)}, bf16[2,128,768]{2,1,0:T(8,128)(2,1)S(1)}, u32[]{:S(2)}, u32[]{:S(2)}) %collective-permute-start.12) | collective-permute-done | bytes 393248 | tf_op jit(solution)/shard_map/ppermute | solution.py:475
  389.5 2.9 input_back.1
  392.3 2.6 broadcast_select_fusion.10
  396.4 3.6 convert_bitcast_fusion
  400.0 8.0 %copy.112 = f32[768,3,768]{0,2,1:T(8,128)} copy(f32[768,3,768]{2,0,1:T(8,128)} %convert_bitcast_fusion) | data formatting | bytes 14155776 | tf_op jit(solution)/shard_map/convert_element_type | solution.py:706
  408.1 8.0 %copy.115 = f32[768,2304]{1,0:T(8,128)} copy(f32[768,2304]{0,1:T(8,128)} %bitcast.181) | data formatting | bytes 14155776
  416.0 3.0 slice_convert_fusion.1
  419.0 3.6 broadcast_select_fusion.3
  422.7 14.4 %pad_maximum_fusion = bf16[6144,768]{1,0:T(8,128)(2,1)S(1)} fusion(bf16[3072,768]{1,0:T(8,128)(2,1)S(1)} %get-tuple-element.145, bf16[3072,768]{1,0:T(8,128)(2,1)S(1)} %get-tuple-element.144), kind=kLoop, calls=%fused_computation.3 | loop fusion | flops 18874368 | bytes 18874368 | tf_op jit(solution)/shard_map/concatenate | solution.py:547
  437.0 6.4 %fusion.31 = (bf16[4,1,768,768]{3,2,1,0:T(8,128)(2,1)}, f32[4,1,768,768]{3,2,1,0:T(8,128)}) fusion(bf16[4,2,768,768]{3,2,1,0:T(8,128)(2,1)S(1)} %bitcast.180), kind=kLoop, calls=%fused_computation.169 | loop fusion | flops 2359296 | bytes 23592960 | tf_op jit(solution)/shard_map/slice | solution.py:704
  443.4 13.5 %copy.128 = f32[4,1,768,768]{3,0,2,1:T(4,128)} copy(f32[4,1,768,768]{3,2,1,0:T(8,128)} %get-tuple-element.143) | data formatting | bytes 18874368
  456.9 9.8 %copy.120 = f32[96,8,4,768]{3,1,2,0:T(8,128)} copy(f32[96,8,4,768]{3,2,1,0:T(4,128)} %bitcast.179) | data formatting | bytes 18874368
  466.7 4.8 %bitcast_convert_fusion = f32[3072,768]{1,0:T(8,128)} fusion(bf16[4,1,768,768]{3,2,1,0:T(8,128)(2,1)S(1)} %bitcast.185), kind=kLoop, calls=%fused_computation.9 | loop fusion | flops 2359296 | bytes 14155776 | tf_op jit(solution)/shard_map/convert_element_type | solution.py:704
  (206 shorter events, 74.0 us)
Async XLA Ops:
  0.6 25.9 %collective-permute-start.2 = (bf16[2,128,768]{2,1,0:T(8,128)(2,1)}, bf16[2,128,768]{2,1,0:T(8,128)(2,1)S(1)}, u32[]{:S(2)}, u32[]{:S(2)}) collective-permute-start(bf16[2,128,768]{2,1,0:T(8,128)(2,1)} %param.17), channel_id=1, source_target_pairs={{0,6},{1,7},{2,4},{3,5},{4,2},{5,3},{6,0},{7,1},{8,14},{9,15},{10,... | collective-permute-start | bytes 1179656 | tf_op jit(solution)/shard_map/ppermute | solution.py:475
  5.8 33.8 %collective-permute-start.1 = (bf16[2,128,768]{2,1,0:T(8,128)(2,1)}, bf16[2,128,768]{2,1,0:T(8,128)(2,1)S(1)}, u32[]{:S(2)}, u32[]{:S(2)}) collective-permute-start(bf16[2,128,768]{2,1,0:T(8,128)(2,1)} %param.17), channel_id=1, source_target_pairs={{0,4},{1,5},{2,6},{3,7},{4,0},{5,1},{6,2},{7,3},{8,12},{9,13},{10,... | collective-permute-start | bytes 1179656 | tf_op jit(solution)/shard_map/ppermute | solution.py:475
  5.8 33.8 %collective-permute-start = (bf16[2,128,768]{2,1,0:T(8,128)(2,1)}, bf16[2,128,768]{2,1,0:T(8,128)(2,1)S(1)}, u32[]{:S(2)}, u32[]{:S(2)}) collective-permute-start(bf16[2,128,768]{2,1,0:T(8,128)(2,1)} %param.17), channel_id=1, source_target_pairs={{0,2},{1,3},{2,0},{3,1},{4,6},{5,7},{6,4},{7,5},{8,10},{9,11},{10,... | collective-permute-start | bytes 1179656 | tf_op jit(solution)/shard_map/ppermute | solution.py:475
  19.4 20.1 %copy-start.11 = (bf16[2,128,768]{2,1,0:T(8,128)(2,1)S(1)}, bf16[2,128,768]{2,1,0:T(8,128)(2,1)}, u32[]{:S(2)}) copy-start(bf16[2,128,768]{2,1,0:T(8,128)(2,1)} %param.17) | copy-start | bytes 1179652
  21.9 33.2 %collective-permute-start.6 = (bf16[2,128,768]{2,1,0:T(8,128)(2,1)}, bf16[2,128,768]{2,1,0:T(8,128)(2,1)}, u32[]{:S(2)}, u32[]{:S(2)}) collective-permute-start(bf16[2,128,768]{2,1,0:T(8,128)(2,1)} %pad_maximum_fusion.12), channel_id=1, source_target_pairs={{0,24},{1,25},{2,26},{3,27},{4,28},{5,29},{6,30},{7,31},{8,16},{9,... | collective-permute-start | bytes 1179656 | tf_op jit(solution)/shard_map/ppermute | solution.py:475
  24.5 16.1 %copy-start.18 = (f32[768]{0:T(1024)S(1)}, f32[768]{0:T(1024)}, u32[]{:S(2)}) copy-start(f32[768]{0:T(1024)} %param.25) | copy-start | bytes 9220
  24.5 16.7 %copy-start.19 = (f32[768]{0:T(1024)S(1)}, f32[768]{0:T(1024)}, u32[]{:S(2)}) copy-start(f32[768]{0:T(1024)} %param.26) | copy-start | bytes 9220
  24.5 17.2 %copy-start.23 = (f32[768]{0:T(1024)S(1)}, f32[768]{0:T(1024)}, u32[]{:S(2)}) copy-start(f32[768]{0:T(1024)} %param.21) | copy-start | bytes 9220
  25.3 29.9 %collective-permute-start.5 = (bf16[2,128,768]{2,1,0:T(8,128)(2,1)}, bf16[2,128,768]{2,1,0:T(8,128)(2,1)}, u32[]{:S(2)}, u32[]{:S(2)}) collective-permute-start(bf16[2,128,768]{2,1,0:T(8,128)(2,1)} %pad_maximum_fusion.11), channel_id=1, source_target_pairs={{0,16},{1,17},{2,18},{3,19},{4,20},{5,21},{6,22},{7,23},{8,24},{9,... | collective-permute-start | bytes 1179656 | tf_op jit(solution)/shard_map/ppermute | solution.py:475
  26.6 28.5 %collective-permute-start.4 = (bf16[2,128,768]{2,1,0:T(8,128)(2,1)}, bf16[2,128,768]{2,1,0:T(8,128)(2,1)}, u32[]{:S(2)}, u32[]{:S(2)}) collective-permute-start(bf16[2,128,768]{2,1,0:T(8,128)(2,1)} %pad_maximum_fusion.10), channel_id=1, source_target_pairs={{0,8},{1,9},{2,10},{3,11},{4,12},{5,13},{6,14},{7,15},{8,0},{9,1},... | collective-permute-start | bytes 1179656 | tf_op jit(solution)/shard_map/ppermute | solution.py:475
  39.7 17.5 %collective-permute-start.3 = (bf16[4,2,128,768]{3,2,1,0:T(8,128)(2,1)S(1)}, bf16[4,2,128,768]{3,2,1,0:T(8,128)(2,1)}, u32[]{:S(2)}, u32[]{:S(2)}) collective-permute-start(bf16[4,2,128,768]{3,2,1,0:T(8,128)(2,1)S(1)} %pad_maximum_fusion.6), channel_id=1, source_target_pairs={{0,1},{1,0},{2,3},{3,2},{4,5},{5,4},{6,7},{7,6},{8,9},{9,8},{10,11... | collective-permute-start | bytes 4718600 | tf_op jit(solution)/shard_map/ppermute | solution.py:475
  111.0 15.7 %collective-permute-start.31 = (bf16[3072,768]{1,0:T(8,128)(2,1)}, bf16[3072,768]{1,0:T(8,128)(2,1)}, u32[]{:S(2)}, u32[]{:S(2)}) collective-permute-start(bf16[3072,768]{1,0:T(8,128)(2,1)} %bitcast.75), channel_id=1, source_target_pairs={{0,1},{1,0},{2,3},{3,2},{4,5},{5,4},{6,7},{7,6},{8,9},{9,8},{10,11... | collective-permute-start | bytes 14155784 | tf_op jit(solution)/shard_map/ppermute | solution.py:475
  111.5 15.2 %slice-start = ((s8[4718592]{0:T(1024)(128)(4,1)}), s8[4194304]{0:T(1024)(128)(4,1)S(1)}, s32[]{:S(2)}) async-start(s8[4718592]{0:T(1024)(128)(4,1)} %bitcast.182), calls=%async_computation | async-start | bytes 8388608
  111.5 15.2 %slice-start.1 = ((s8[4718592]{0:T(1024)(128)(4,1)}), s8[524288]{0:T(1024)(128)(4,1)S(1)}, s32[]{:S(2)}) async-start(s8[4718592]{0:T(1024)(128)(4,1)} %bitcast.182), calls=%async_computation.1 | async-start | bytes 1048576
  130.2 2.2 copy-start.1
  132.4 28.9 %collective-permute-start.32 = (bf16[1536,768]{1,0:T(8,128)(2,1)S(1)}, bf16[1536,768]{1,0:T(8,128)(2,1)}, u32[]{:S(2)}, u32[]{:S(2)}) collective-permute-start(bf16[1536,768]{1,0:T(8,128)(2,1)S(1)} %broadcast_select_fusion.6), channel_id=1, source_target_pairs={{0,8},{1,17},{2,10},{3,19},{4,12},{5,21},{6,14},{7,23},{8,0},{9,25... | collective-permute-start | bytes 7077896 | tf_op jit(solution)/shard_map/ppermute | solution.py:475
  133.9 17.9 %copy-start.14 = (bf16[768,768]{1,0:T(8,128)(2,1)S(1)}, bf16[768,768]{1,0:T(8,128)(2,1)}, u32[]{:S(2)}) copy-start(bf16[768,768]{1,0:T(8,128)(2,1)} %get-tuple-element.60) | copy-start | bytes 3538948
  156.4 10.6 %collective-permute-start.14 = (bf16[1536,768]{1,0:T(8,128)(2,1)}, bf16[1536,768]{1,0:T(8,128)(2,1)}, u32[]{:S(2)}, u32[]{:S(2)}) collective-permute-start(bf16[1536,768]{1,0:T(8,128)(2,1)} %bitcast.60), channel_id=1, source_target_pairs={{0,1},{1,0},{2,3},{3,2},{4,5},{5,4},{6,7},{7,6},{8,9},{9,8},{10,11... | collective-permute-start | bytes 7077896 | tf_op jit(solution)/shard_map/ppermute | solution.py:475
  165.3 4.8 %copy-start.2 = (bf16[1536,768]{1,0:T(8,128)(2,1)}, bf16[1536,768]{1,0:T(8,128)(2,1)S(1)}, u32[]{:S(2)}) copy-start(bf16[1536,768]{1,0:T(8,128)(2,1)S(1)} %add_convert_fusion) | copy-start | bytes 7077892
  165.3 2.5 copy-start.10
  165.5 24.8 %collective-permute-start.33 = (bf16[768,768]{1,0:T(8,128)(2,1)S(1)}, bf16[768,768]{1,0:T(8,128)(2,1)}, u32[]{:S(2)}, u32[]{:S(2)}) collective-permute-start(bf16[768,768]{1,0:T(8,128)(2,1)S(1)} %broadcast_select_fusion.13), channel_id=1, source_target_pairs={{0,16},{1,9},{2,18},{3,11},{4,20},{5,13},{6,22},{7,15},{8,24},{9,1... | collective-permute-start | bytes 3538952 | tf_op jit(solution)/shard_map/ppermute | solution.py:475
  171.2 48.5 %collective-permute-start.15 = (bf16[768,768]{1,0:T(8,128)(2,1)}, bf16[768,768]{1,0:T(8,128)(2,1)}, u32[]{:S(2)}, u32[]{:S(2)}) collective-permute-start(bf16[768,768]{1,0:T(8,128)(2,1)} %broadcast_select_fusion.16), channel_id=1, source_target_pairs={{0,8},{1,17},{2,10},{3,19},{4,12},{5,21},{6,14},{7,23},{8,0},{9,25... | collective-permute-start | bytes 3538952 | tf_op jit(solution)/shard_map/ppermute | solution.py:475
  193.6 12.1 %collective-permute-start.36 = (bf16[192,768]{1,0:T(8,128)(2,1)}, bf16[192,768]{1,0:T(8,128)(2,1)}, u32[]{:S(2)}, u32[]{:S(2)}) collective-permute-start(bf16[192,768]{1,0:T(8,128)(2,1)} %get-tuple-element.168), channel_id=1, source_target_pairs={{0,6},{1,7},{2,4},{3,5},{4,2},{5,3},{6,0},{7,1},{8,14},{9,15},{10,... | collective-permute-start | bytes 884744 | tf_op jit(solution)/shard_map/ppermute | solution.py:475
  196.1 19.6 %collective-permute-start.35 = (bf16[192,768]{1,0:T(8,128)(2,1)}, bf16[192,768]{1,0:T(8,128)(2,1)}, u32[]{:S(2)}, u32[]{:S(2)}) collective-permute-start(bf16[192,768]{1,0:T(8,128)(2,1)} %get-tuple-element.169), channel_id=1, source_target_pairs={{0,4},{1,5},{2,6},{3,7},{4,0},{5,1},{6,2},{7,3},{8,12},{9,13},{10,... | collective-permute-start | bytes 884744 | tf_op jit(solution)/shard_map/ppermute | solution.py:475
  196.1 19.6 %collective-permute-start.34 = (bf16[192,768]{1,0:T(8,128)(2,1)}, bf16[192,768]{1,0:T(8,128)(2,1)}, u32[]{:S(2)}, u32[]{:S(2)}) collective-permute-start(bf16[192,768]{1,0:T(8,128)(2,1)} %get-tuple-element.167), channel_id=1, source_target_pairs={{0,2},{1,3},{2,0},{3,1},{4,6},{5,7},{6,4},{7,5},{8,10},{9,11},{10,... | collective-permute-start | bytes 884744 | tf_op jit(solution)/shard_map/ppermute | solution.py:475
  217.1 13.5 %collective-permute-start.37 = (bf16[192,768]{1,0:T(8,128)(2,1)S(1)}, bf16[192,768]{1,0:T(8,128)(2,1)S(1)}, u32[]{:S(2)}, u32[]{:S(2)}) collective-permute-start(bf16[192,768]{1,0:T(8,128)(2,1)S(1)} %get-tuple-element.138), channel_id=1, source_target_pairs={{0,2},{1,3},{2,0},{3,1},{4,6},{5,7},{6,4},{7,5},{8,10},{9,11},{10,... | collective-permute-start | bytes 884744 | tf_op jit(solution)/shard_map/ppermute | solution.py:475
  217.2 22.1 %collective-permute-start.38 = (bf16[192,768]{1,0:T(8,128)(2,1)S(1)}, bf16[192,768]{1,0:T(8,128)(2,1)S(1)}, u32[]{:S(2)}, u32[]{:S(2)}) collective-permute-start(bf16[192,768]{1,0:T(8,128)(2,1)S(1)} %get-tuple-element.138), channel_id=1, source_target_pairs={{0,4},{1,5},{2,6},{3,7},{4,0},{5,1},{6,2},{7,3},{8,12},{9,13},{10,... | collective-permute-start | bytes 884744 | tf_op jit(solution)/shard_map/ppermute | solution.py:475
  221.4 17.8 %collective-permute-start.39 = (bf16[192,768]{1,0:T(8,128)(2,1)S(1)}, bf16[192,768]{1,0:T(8,128)(2,1)S(1)}, u32[]{:S(2)}, u32[]{:S(2)}) collective-permute-start(bf16[192,768]{1,0:T(8,128)(2,1)S(1)} %get-tuple-element.138), channel_id=1, source_target_pairs={{0,6},{1,7},{2,4},{3,5},{4,2},{5,3},{6,0},{7,1},{8,14},{9,15},{10,... | collective-permute-start | bytes 884744 | tf_op jit(solution)/shard_map/ppermute | solution.py:475
  239.3 29.0 %collective-permute-start.40 = (bf16[768,768]{1,0:T(8,128)(2,1)S(1)}, bf16[768,768]{1,0:T(8,128)(2,1)S(1)}, u32[]{:S(2)}, u32[]{:S(2)}) collective-permute-start(bf16[768,768]{1,0:T(8,128)(2,1)S(1)} %bitcast.194), channel_id=1, source_target_pairs={{0,16},{1,9},{2,18},{3,11},{4,20},{5,13},{6,22},{7,15},{8,24},{9,1... | collective-permute-start | bytes 3538952 | tf_op jit(solution)/shard_map/ppermute | solution.py:475
  241.0 20.9 %collective-permute-start.16 = (bf16[384,768]{1,0:T(8,128)(2,1)S(1)}, bf16[384,768]{1,0:T(8,128)(2,1)S(1)}, u32[]{:S(2)}, u32[]{:S(2)}) collective-permute-start(bf16[384,768]{1,0:T(8,128)(2,1)S(1)} %broadcast_select_fusion.19), channel_id=1, source_target_pairs={{0,16},{1,9},{2,18},{3,11},{4,20},{5,13},{6,22},{7,15},{8,24},{9,1... | collective-permute-start | bytes 1769480 | tf_op jit(solution)/shard_map/ppermute | solution.py:475
  262.2 9.7 %collective-permute-start.19 = (bf16[96,768]{1,0:T(8,128)(2,1)S(1)}, bf16[96,768]{1,0:T(8,128)(2,1)S(1)}, u32[]{:S(2)}, u32[]{:S(2)}) collective-permute-start(bf16[96,768]{1,0:T(8,128)(2,1)S(1)} %get-tuple-element.181), channel_id=1, source_target_pairs={{0,6},{1,7},{2,4},{3,5},{4,2},{5,3},{6,0},{7,1},{8,14},{9,15},{10,... | collective-permute-start | bytes 442376 | tf_op jit(solution)/shard_map/ppermute | solution.py:475
  264.6 12.4 %collective-permute-start.18 = (bf16[96,768]{1,0:T(8,128)(2,1)S(1)}, bf16[96,768]{1,0:T(8,128)(2,1)S(1)}, u32[]{:S(2)}, u32[]{:S(2)}) collective-permute-start(bf16[96,768]{1,0:T(8,128)(2,1)S(1)} %get-tuple-element.182), channel_id=1, source_target_pairs={{0,4},{1,5},{2,6},{3,7},{4,0},{5,1},{6,2},{7,3},{8,12},{9,13},{10,... | collective-permute-start | bytes 442376 | tf_op jit(solution)/shard_map/ppermute | solution.py:475
  268.3 8.7 %collective-permute-start.17 = (bf16[96,768]{1,0:T(8,128)(2,1)S(1)}, bf16[96,768]{1,0:T(8,128)(2,1)S(1)}, u32[]{:S(2)}, u32[]{:S(2)}) collective-permute-start(bf16[96,768]{1,0:T(8,128)(2,1)S(1)} %get-tuple-element.180), channel_id=1, source_target_pairs={{0,2},{1,3},{2,0},{3,1},{4,6},{5,7},{6,4},{7,5},{8,10},{9,11},{10,... | collective-permute-start | bytes 442376 | tf_op jit(solution)/shard_map/ppermute | solution.py:475
  268.6 1.8 copy-start.8
  270.3 22.7 %copy-start = (s32[8]{0:T(128)S(1)}, s32[8]{0:T(128)}, u32[]{:S(2)}) copy-start(s32[8]{0:T(128)} %param.18) | copy-start | bytes 100
  270.3 35.5 %collective-permute-start.41 = (bf16[1536,768]{1,0:T(8,128)(2,1)}, bf16[1536,768]{1,0:T(8,128)(2,1)}, u32[]{:S(2)}, u32[]{:S(2)}) collective-permute-start(bf16[1536,768]{1,0:T(8,128)(2,1)} %pad_maximum_fusion.5), channel_id=1, source_target_pairs={{0,8},{1,17},{2,10},{3,19},{4,12},{5,21},{6,14},{7,23},{8,0},{9,25... | collective-permute-start | bytes 7077896 | tf_op jit(solution)/shard_map/ppermute | solution.py:475
  277.1 6.8 %collective-permute-start.20 = (bf16[96,768]{1,0:T(8,128)(2,1)S(1)}, bf16[96,768]{1,0:T(8,128)(2,1)S(1)}, u32[]{:S(2)}, u32[]{:S(2)}) collective-permute-start(bf16[96,768]{1,0:T(8,128)(2,1)S(1)} %get-tuple-element.140), channel_id=1, source_target_pairs={{0,2},{1,3},{2,0},{3,1},{4,6},{5,7},{6,4},{7,5},{8,10},{9,11},{10,... | collective-permute-start | bytes 442376 | tf_op jit(solution)/shard_map/ppermute | solution.py:475
  277.3 13.4 %collective-permute-start.21 = (bf16[96,768]{1,0:T(8,128)(2,1)S(1)}, bf16[96,768]{1,0:T(8,128)(2,1)S(1)}, u32[]{:S(2)}, u32[]{:S(2)}) collective-permute-start(bf16[96,768]{1,0:T(8,128)(2,1)S(1)} %get-tuple-element.140), channel_id=1, source_target_pairs={{0,4},{1,5},{2,6},{3,7},{4,0},{5,1},{6,2},{7,3},{8,12},{9,13},{10,... | collective-permute-start | bytes 442376 | tf_op jit(solution)/shard_map/ppermute | solution.py:475
  279.1 11.7 %collective-permute-start.22 = (bf16[96,768]{1,0:T(8,128)(2,1)S(1)}, bf16[96,768]{1,0:T(8,128)(2,1)S(1)}, u32[]{:S(2)}, u32[]{:S(2)}) collective-permute-start(bf16[96,768]{1,0:T(8,128)(2,1)S(1)} %get-tuple-element.140), channel_id=1, source_target_pairs={{0,6},{1,7},{2,4},{3,5},{4,2},{5,3},{6,0},{7,1},{8,14},{9,15},{10,... | collective-permute-start | bytes 442376 | tf_op jit(solution)/shard_map/ppermute | solution.py:475
  290.8 10.4 %collective-permute-start.23 = (bf16[384,768]{1,0:T(8,128)(2,1)S(1)}, bf16[384,768]{1,0:T(8,128)(2,1)S(1)}, u32[]{:S(2)}, u32[]{:S(2)}) collective-permute-start(bf16[384,768]{1,0:T(8,128)(2,1)S(1)} %bitcast.197), channel_id=1, source_target_pairs={{0,16},{1,9},{2,18},{3,11},{4,20},{5,13},{6,22},{7,15},{8,24},{9,1... | collective-permute-start | bytes 1769480 | tf_op jit(solution)/shard_map/ppermute | solution.py:475
  298.9 51.9 %collective-permute-start.10 = (bf16[2,4,128,768]{3,2,0,1:T(8,128)(2,1)}, bf16[2,4,128,768]{3,2,0,1:T(8,128)(2,1)}, u32[]{:S(2)}, u32[]{:S(2)}) collective-permute-start(bf16[2,4,128,768]{3,2,0,1:T(8,128)(2,1)} %bitcast.177), channel_id=1, source_target_pairs={{0,1},{1,0},{2,3},{3,2},{4,5},{5,4},{6,7},{7,6},{8,9},{9,8},{10,11... | collective-permute-start | bytes 4718600 | tf_op jit(solution)/shard_map/ppermute | solution.py:475
  299.0 6.8 %copy-start.9 = (bf16[768,768]{1,0:T(8,128)(2,1)S(1)}, bf16[768,768]{1,0:T(8,128)(2,1)}, u32[]{:S(2)}) copy-start(bf16[768,768]{1,0:T(8,128)(2,1)} %copy-done.8) | copy-start | bytes 3538948
  299.0 4.1 collective-permute-start.26
  301.4 16.9 %collective-permute-start.24 = (bf16[768,768]{1,0:T(8,128)(2,1)S(1)}, bf16[768,768]{1,0:T(8,128)(2,1)S(1)}, u32[]{:S(2)}, u32[]{:S(2)}) collective-permute-start(bf16[768,768]{1,0:T(8,128)(2,1)S(1)} %pad_maximum_fusion.8), channel_id=1, source_target_pairs={{0,8},{1,17},{2,10},{3,19},{4,12},{5,21},{6,14},{7,23},{8,0},{9,25... | collective-permute-start | bytes 3538952 | tf_op jit(solution)/shard_map/ppermute | solution.py:475
  303.1 18.1 %collective-permute-start.27 = (f32[12,768]{1,0:T(8,128)S(1)}, f32[12,768]{1,0:T(8,128)S(1)}, u32[]{:S(2)}, u32[]{:S(2)}) collective-permute-start(f32[12,768]{1,0:T(8,128)S(1)} %fusion.28), channel_id=1, source_target_pairs={{0,2},{1,3},{2,0},{3,1},{4,6},{5,7},{6,4},{7,5},{8,10},{9,11},{10,... | collective-permute-start | bytes 110600 | tf_op jit(solution)/shard_map/ppermute | solution.py:475
  308.5 2.9 copy-start.3
  311.4 107.6 %collective-permute-start.42 = (bf16[3072,768]{1,0:T(8,128)(2,1)}, bf16[3072,768]{1,0:T(8,128)(2,1)}, u32[]{:S(2)}, u32[]{:S(2)}) collective-permute-start(bf16[3072,768]{1,0:T(8,128)(2,1)} %pad_maximum_fusion.1), channel_id=1, source_target_pairs={{0,1},{1,0},{2,3},{3,2},{4,5},{5,4},{6,7},{7,6},{8,9},{9,8},{10,11... | collective-permute-start | bytes 14155784 | tf_op jit(solution)/shard_map/ppermute | solution.py:475
  318.8 1.7 copy-start.6
  320.5 71.8 %collective-permute-start.25 = (bf16[1536,768]{1,0:T(8,128)(2,1)}, bf16[1536,768]{1,0:T(8,128)(2,1)}, u32[]{:S(2)}, u32[]{:S(2)}) collective-permute-start(bf16[1536,768]{1,0:T(8,128)(2,1)} %pad_maximum_fusion.4), channel_id=1, source_target_pairs={{0,1},{1,0},{2,3},{3,2},{4,5},{5,4},{6,7},{7,6},{8,9},{9,8},{10,11... | collective-permute-start | bytes 7077896 | tf_op jit(solution)/shard_map/ppermute | solution.py:475
  321.2 6.2 %collective-permute-start.28 = (f32[12,768]{1,0:T(8,128)S(1)}, f32[12,768]{1,0:T(8,128)S(1)}, u32[]{:S(2)}, u32[]{:S(2)}) collective-permute-start(f32[12,768]{1,0:T(8,128)S(1)} %add.525), channel_id=1, source_target_pairs={{0,4},{1,5},{2,6},{3,7},{4,0},{5,1},{6,2},{7,3},{8,12},{9,13},{10,... | collective-permute-start | bytes 110600 | tf_op jit(solution)/shard_map/ppermute | solution.py:475
  327.4 4.2 collective-permute-start.29
  332.1 12.0 %collective-permute-start.30 = (f32[12,768]{1,0:T(8,128)}, f32[12,768]{1,0:T(8,128)}, u32[]{:S(2)}, u32[]{:S(2)}) collective-permute-start(f32[12,768]{1,0:T(8,128)} %add.527), channel_id=1, source_target_pairs={{0,16},{1,17},{2,18},{3,19},{4,20},{5,21},{6,22},{7,23},{8,24},{9,... | collective-permute-start | bytes 110600 | tf_op jit(solution)/shard_map/ppermute | solution.py:475
  342.4 11.7 %collective-permute-start.9 = (bf16[2,128,768]{2,1,0:T(8,128)(2,1)}, bf16[2,128,768]{2,1,0:T(8,128)(2,1)}, u32[]{:S(2)}, u32[]{:S(2)}) collective-permute-start(bf16[2,128,768]{2,1,0:T(8,128)(2,1)} %bitcast.205), channel_id=1, source_target_pairs={{0,24},{1,25},{2,26},{3,27},{4,28},{5,29},{6,30},{7,31},{8,16},{9,... | collective-permute-start | bytes 1179656 | tf_op jit(solution)/shard_map/ppermute | solution.py:475
  344.2 16.7 %collective-permute-start.8 = (bf16[2,128,768]{2,1,0:T(8,128)(2,1)}, bf16[2,128,768]{2,1,0:T(8,128)(2,1)}, u32[]{:S(2)}, u32[]{:S(2)}) collective-permute-start(bf16[2,128,768]{2,1,0:T(8,128)(2,1)} %bitcast.206), channel_id=1, source_target_pairs={{0,16},{1,17},{2,18},{3,19},{4,20},{5,21},{6,22},{7,23},{8,24},{9,... | collective-permute-start | bytes 1179656 | tf_op jit(solution)/shard_map/ppermute | solution.py:475
  349.5 3.9 copy-start.17
  350.8 12.8 %collective-permute-start.7 = (bf16[2,128,768]{2,1,0:T(8,128)(2,1)}, bf16[2,128,768]{2,1,0:T(8,128)(2,1)S(1)}, u32[]{:S(2)}, u32[]{:S(2)}) collective-permute-start(bf16[2,128,768]{2,1,0:T(8,128)(2,1)} %bitcast.207), channel_id=1, source_target_pairs={{0,8},{1,9},{2,10},{3,11},{4,12},{5,13},{6,14},{7,15},{8,0},{9,1},... | collective-permute-start | bytes 1179656 | tf_op jit(solution)/shard_map/ppermute | solution.py:475
  353.4 10.4 %copy-start.15 = (bf16[256,768]{1,0:T(8,128)(2,1)S(1)}, bf16[256,768]{1,0:T(8,128)(2,1)}, u32[]{:S(2)}) copy-start(bf16[256,768]{1,0:T(8,128)(2,1)} %get-tuple-element.44) | copy-start | bytes 1179652
  354.1 14.6 %collective-permute-start.13 = (bf16[2,128,768]{2,1,0:T(8,128)(2,1)S(1)}, bf16[2,128,768]{2,1,0:T(8,128)(2,1)S(1)}, u32[]{:S(2)}, u32[]{:S(2)}) collective-permute-start(bf16[2,128,768]{2,1,0:T(8,128)(2,1)S(1)} %get-tuple-element.161), channel_id=1, source_target_pairs={{0,6},{1,7},{2,4},{3,5},{4,2},{5,3},{6,0},{7,1},{8,14},{9,15},{10,... | collective-permute-start | bytes 1179656 | tf_op jit(solution)/shard_map/ppermute | solution.py:475
  360.9 27.6 %collective-permute-start.12 = (bf16[2,128,768]{2,1,0:T(8,128)(2,1)S(1)}, bf16[2,128,768]{2,1,0:T(8,128)(2,1)S(1)}, u32[]{:S(2)}, u32[]{:S(2)}) collective-permute-start(bf16[2,128,768]{2,1,0:T(8,128)(2,1)S(1)} %get-tuple-element.162), channel_id=1, source_target_pairs={{0,4},{1,5},{2,6},{3,7},{4,0},{5,1},{6,2},{7,3},{8,12},{9,13},{10,... | collective-permute-start | bytes 1179656 | tf_op jit(solution)/shard_map/ppermute | solution.py:475
  363.5 25.0 %collective-permute-start.11 = (bf16[2,128,768]{2,1,0:T(8,128)(2,1)S(1)}, bf16[2,128,768]{2,1,0:T(8,128)(2,1)S(1)}, u32[]{:S(2)}, u32[]{:S(2)}) collective-permute-start(bf16[2,128,768]{2,1,0:T(8,128)(2,1)S(1)} %get-tuple-element.160), channel_id=1, source_target_pairs={{0,2},{1,3},{2,0},{3,1},{4,6},{5,7},{6,4},{7,5},{8,10},{9,11},{10,... | collective-permute-start | bytes 1179656 | tf_op jit(solution)/shard_map/ppermute | solution.py:475
  368.7 23.7 %copy-start.7 = (bf16[768,768]{1,0:T(8,128)(2,1)S(1)}, bf16[768,768]{1,0:T(8,128)(2,1)}, u32[]{:S(2)}) copy-start(bf16[768,768]{1,0:T(8,128)(2,1)} %copy-done.6) | copy-start | bytes 3538948
  416.0 3.0 copy-start.4
  443.4 23.3 %slice-start.2 = ((s8[4718592]{0:T(1024)(128)(4,1)}), s8[524288]{0:T(1024)(128)(4,1)S(1)}, s32[]{:S(2)}) async-start(s8[4718592]{0:T(1024)(128)(4,1)} %bitcast.184), calls=%async_computation.2 | async-start | bytes 1048576
  456.9 9.8 %slice-start.3 = ((s8[4718592]{0:T(1024)(128)(4,1)}), s8[4194304]{0:T(1024)(128)(4,1)S(1)}, s32[]{:S(2)}) async-start(s8[4718592]{0:T(1024)(128)(4,1)} %bitcast.184), calls=%async_computation.3 | async-start | bytes 8388608
  (7 other events, 8.6 us)
